TPU v7x, 512 devices: a whole 4x4x16 slice. The times are simulated.
512 devices in a mesh: row: 16 (over x, y), col: 16 (over z), layer: 2 (over core).
Axes of the slice: x: 4, y: 4, z: 16, core: 2. Of those that a mesh axis runs over, the one named last changes fastest.
Arguments:
- density: bfloat16 [6144, 6144], P('row', 'col'), may hold values from -1 to 1.5, as said below
- product_pattern: int32 [96, 96], P('row', 'col'), may hold values from 0 to 1, as said below
Outputs:
- purified: bfloat16 [6144, 6144], P(('row', 'layer'), 'col')
Inputs may be any that keep to these rules, and one draw needn't show every extreme that they name: `density`: symmetric; zero outside a symmetric pattern of 64 x 64 tiles that holds every diagonal tile. `product_pattern`: 0 or 1; symmetric; every diagonal tile is 1.
All inputs are finite; a program needn't handle non-finite values.
Results may differ from a plain program's by a relative error of at most 0.006.
Values may be sent and summed in bfloat16 or wider, within the bound.
No kernel may reach another device: no remote copies, remote signals or barrier semaphores. Data moves between devices by JAX's collectives and lax.ppermute only.
A program may use at most 64 MiB of HBM per device.

v0:
```python
import jax
import jax.numpy as jnp
from jax import lax
from jax.sharding import PartitionSpec as P

TILE = 64


def passed_along(block, axis, distance):
    devices = range(lax.axis_size(axis))
    route = [((i - distance) % len(devices), i) for i in devices]
    return lax.ppermute(block, axis, route)


def expand_tiles(tile_mask):
    tile_rows, tile_cols = tile_mask.shape
    tile_grid = tile_mask.astype(jnp.float32)[:, None, :, None]
    return jnp.broadcast_to(tile_grid, (tile_rows, TILE, tile_cols, TILE)).reshape(
        tile_rows * TILE, tile_cols * TILE
    )


def skew_left_blocks(left_block, amount):
    bit_count = lax.axis_size("col").bit_length() - 1
    for which_bit in range(bit_count):
        arrived = passed_along(left_block, "col", -(1 << which_bit))
        left_block = jnp.where(amount >> which_bit & 1 == 1, arrived, left_block)
    return left_block


def skew_right_blocks(right_block, amount):
    bit_count = lax.axis_size("row").bit_length() - 1
    for which_bit in range(bit_count):
        arrived = passed_along(right_block, "row", -(1 << which_bit))
        right_block = jnp.where(amount >> which_bit & 1 == 1, arrived, right_block)
    return right_block


def multiply(left_block, right_block, offset, steps_each):
    grid_side = lax.axis_size("row")
    left_block = skew_left_blocks(left_block, (lax.axis_index("row") + offset) % grid_side)
    running = jnp.dot(left_block, right_block, preferred_element_type=jnp.float32)

    def advance(step_index, state_tuple):
        running, left_now, right_now = state_tuple
        left_now = passed_along(left_now, "col", -1)
        right_now = passed_along(right_now, "row", -1)
        running = running + jnp.dot(left_now, right_now, preferred_element_type=jnp.float32)
        return (running, left_now, right_now)

    running, _, _ = lax.fori_loop(1, steps_each, advance, (running, left_block, right_block))
    return running


def shards(density, product_pattern):
    grid_side = lax.axis_size("row")
    layers = lax.axis_size("layer")
    layer_pos = lax.axis_index("layer")
    block_rows = density.shape[0]
    half_rows = block_rows // layers
    mask_rows = lax.dynamic_slice_in_dim(
        product_pattern, layer_pos * (half_rows // TILE), half_rows // TILE, 0
    )
    steps_each = grid_side // layers
    offset = layer_pos * steps_each
    right_start = skew_right_blocks(density, (lax.axis_index("col") + offset) % grid_side)
    partial_value = multiply(density, right_start, offset, steps_each)
    summed = lax.psum(partial_value, "layer")
    squared = (summed * expand_tiles(product_pattern)).astype(jnp.bfloat16)
    partial_value = multiply(squared, right_start, offset, steps_each)
    cubed_part = lax.psum_scatter(partial_value, "layer", scatter_dimension=0, tiled=True)
    square_rows = lax.dynamic_slice_in_dim(squared, layer_pos * half_rows, half_rows, 0)
    result = (3.0 * square_rows.astype(jnp.float32) - 2.0 * cubed_part) * expand_tiles(mask_rows)
    return result.astype(jnp.bfloat16)


def solution(mesh):
    placed = (P("row", "col"), P("row", "col"))
    return jax.shard_map(
        shards, mesh=mesh, in_specs=placed, out_specs=P(("row", "layer"), "col"), check_vma=False
    )
```

profile of v0, /device:TPU:1, one launch (start us, length us, event | category | flops | bytes accessed | tf_op | source)
XLA Modules:
  0.0 500.3 jit_solution(15010346247946394390)
XLA Ops:
  6.5 11.9 %collective-permute-start.4 = (bf16[384,384]{1,0:T(8,128)(2,1)}, bf16[384,384]{1,0:T(8,128)(2,1)S(1)}, u32[]{:S(2)}, u32[]{:S(2)}) collective-permute-start(bf16[384,384]{1,0:T(8,128)(2,1)} %param.6), channel_id=1, source_target_pairs={{2,0},{4,2},{6,4},{8,6},{10,8},{12,10},{14,12},{16,14},{18,16},{20... | collective-permute-start | bytes 884744 | tf_op jit(solution)/shard_map/ppermute | solution.py:12
  18.5 6.8 %collective-permute-start.8 = (bf16[384,384]{1,0:T(8,128)(2,1)}, bf16[384,384]{1,0:T(8,128)(2,1)S(1)}, u32[]{:S(2)}, u32[]{:S(2)}) collective-permute-start(bf16[384,384]{1,0:T(8,128)(2,1)} %param.6), channel_id=1, source_target_pairs={{32,0},{64,32},{96,64},{128,96},{160,128},{192,160},{224,192},{256... | collective-permute-start | bytes 884744 | tf_op jit(solution)/shard_map/ppermute | solution.py:12
  25.4 5.6 %collective-permute-done.8 = bf16[384,384]{1,0:T(8,128)(2,1)S(1)} collective-permute-done((bf16[384,384]{1,0:T(8,128)(2,1)}, bf16[384,384]{1,0:T(8,128)(2,1)S(1)}, u32[]{:S(2)}, u32[]{:S(2)}) %collective-permute-start.8) | collective-permute-done | bytes 294944 | tf_op jit(solution)/shard_map/ppermute | solution.py:12
  49.9 6.3 %collective-permute-start.6 = (bf16[384,384]{1,0:T(8,128)(2,1)S(1)}, bf16[384,384]{1,0:T(8,128)(2,1)S(1)}, u32[]{:S(2)}, u32[]{:S(2)}) collective-permute-start(bf16[384,384]{1,0:T(8,128)(2,1)S(1)} %broadcast_select_fusion.7), channel_id=1, source_target_pairs={{8,0},{10,2},{12,4},{14,6},{16,8},{18,10},{20,12},{22,14},{24,16},... | collective-permute-start | bytes 884744 | tf_op jit(solution)/shard_map/ppermute | solution.py:12
  58.7 11.5 %collective-permute-done.6 = bf16[384,384]{1,0:T(8,128)(2,1)S(1)} collective-permute-done((bf16[384,384]{1,0:T(8,128)(2,1)S(1)}, bf16[384,384]{1,0:T(8,128)(2,1)S(1)}, u32[]{:S(2)}, u32[]{:S(2)}) %collective-permute-start.6) | collective-permute-done | bytes 294944 | tf_op jit(solution)/shard_map/ppermute | solution.py:12
  74.8 20.4 %collective-permute-done.7 = bf16[384,384]{1,0:T(8,128)(2,1)S(1)} collective-permute-done((bf16[384,384]{1,0:T(8,128)(2,1)S(1)}, bf16[384,384]{1,0:T(8,128)(2,1)S(1)}, u32[]{:S(2)}, u32[]{:S(2)}) %collective-permute-start.7) | collective-permute-done | bytes 294944 | tf_op jit(solution)/shard_map/ppermute | solution.py:12
  95.6 122.6 %while.28 = (s32[]{:T(128)}, f32[384,384]{1,0:T(8,128)S(1)}, bf16[384,384]{1,0:T(8,128)(2,1)S(1)}, bf16[384,384]{1,0:T(8,128)(2,1)S(1)}, s32[]{:T(128)}) while((s32[]{:T(128)}, f32[384,384]{1,0:T(8,128)S(1)}, bf16[384,384]{1,0:T(8,128)(2,1)S(1)}, bf16[384,384]{1,0:T(8,128)(2,1)S(1)}, s32[]{:T(128)}) %tuple.32), condition=%wide.region_1.2_spmd, body=%wide.region_0.1_spmd.sunk | while | flops 113393664 | bytes 5308557 | solution.py:51
  95.7 23.5 %collective-permute-start = (bf16[384,384]{1,0:T(8,128)(2,1)S(1)}, bf16[384,384]{1,0:T(8,128)(2,1)S(1)}, u32[]{:S(2)}, u32[]{:S(2)}) collective-permute-start(bf16[384,384]{1,0:T(8,128)(2,1)S(1)} %get-tuple-element.126), channel_id=1, source_target_pairs={{2,0},{4,2},{6,4},{8,6},{10,8},{12,10},{14,12},{16,14},{18,16},{20... | collective-permute-start | bytes 884744 | tf_op jit(solution)/shard_map/while/body/eval_jaxpr/ppermute | solution.py:12
  124.7 6.3 %collective-permute-done.1 = bf16[384,384]{1,0:T(8,128)(2,1)S(1)} collective-permute-done((bf16[384,384]{1,0:T(8,128)(2,1)S(1)}, bf16[384,384]{1,0:T(8,128)(2,1)S(1)}, u32[]{:S(2)}, u32[]{:S(2)}) %collective-permute-start.1) | collective-permute-done | bytes 294944 | tf_op jit(solution)/shard_map/while/body/eval_jaxpr/ppermute | solution.py:12
  144.9 7.4 %collective-permute-start.1 = (bf16[384,384]{1,0:T(8,128)(2,1)S(1)}, bf16[384,384]{1,0:T(8,128)(2,1)S(1)}, u32[]{:S(2)}, u32[]{:S(2)}) collective-permute-start(bf16[384,384]{1,0:T(8,128)(2,1)S(1)} %get-tuple-element.127), channel_id=1, source_target_pairs={{32,0},{64,32},{96,64},{128,96},{160,128},{192,160},{224,192},{256... | collective-permute-start | bytes 884744 | tf_op jit(solution)/shard_map/while/body/eval_jaxpr/ppermute | solution.py:12
  158.4 7.1 %collective-permute-start.1 = (bf16[384,384]{1,0:T(8,128)(2,1)S(1)}, bf16[384,384]{1,0:T(8,128)(2,1)S(1)}, u32[]{:S(2)}, u32[]{:S(2)}) collective-permute-start(bf16[384,384]{1,0:T(8,128)(2,1)S(1)} %get-tuple-element.127), channel_id=1, source_target_pairs={{32,0},{64,32},{96,64},{128,96},{160,128},{192,160},{224,192},{256... | collective-permute-start | bytes 884744 | tf_op jit(solution)/shard_map/while/body/eval_jaxpr/ppermute | solution.py:12
  170.1 9.7 %collective-permute-start = (bf16[384,384]{1,0:T(8,128)(2,1)S(1)}, bf16[384,384]{1,0:T(8,128)(2,1)S(1)}, u32[]{:S(2)}, u32[]{:S(2)}) collective-permute-start(bf16[384,384]{1,0:T(8,128)(2,1)S(1)} %get-tuple-element.126), channel_id=1, source_target_pairs={{2,0},{4,2},{6,4},{8,6},{10,8},{12,10},{14,12},{16,14},{18,16},{20... | collective-permute-start | bytes 884744 | tf_op jit(solution)/shard_map/while/body/eval_jaxpr/ppermute | solution.py:12
  179.8 7.1 %collective-permute-start.1 = (bf16[384,384]{1,0:T(8,128)(2,1)S(1)}, bf16[384,384]{1,0:T(8,128)(2,1)S(1)}, u32[]{:S(2)}, u32[]{:S(2)}) collective-permute-start(bf16[384,384]{1,0:T(8,128)(2,1)S(1)} %get-tuple-element.127), channel_id=1, source_target_pairs={{32,0},{64,32},{96,64},{128,96},{160,128},{192,160},{224,192},{256... | collective-permute-start | bytes 884744 | tf_op jit(solution)/shard_map/while/body/eval_jaxpr/ppermute | solution.py:12
  193.6 7.1 %collective-permute-start.1 = (bf16[384,384]{1,0:T(8,128)(2,1)S(1)}, bf16[384,384]{1,0:T(8,128)(2,1)S(1)}, u32[]{:S(2)}, u32[]{:S(2)}) collective-permute-start(bf16[384,384]{1,0:T(8,128)(2,1)S(1)} %get-tuple-element.127), channel_id=1, source_target_pairs={{32,0},{64,32},{96,64},{128,96},{160,128},{192,160},{224,192},{256... | collective-permute-start | bytes 884744 | tf_op jit(solution)/shard_map/while/body/eval_jaxpr/ppermute | solution.py:12
  207.1 7.1 %collective-permute-start.1 = (bf16[384,384]{1,0:T(8,128)(2,1)S(1)}, bf16[384,384]{1,0:T(8,128)(2,1)S(1)}, u32[]{:S(2)}, u32[]{:S(2)}) collective-permute-start(bf16[384,384]{1,0:T(8,128)(2,1)S(1)} %get-tuple-element.127), channel_id=1, source_target_pairs={{32,0},{64,32},{96,64},{128,96},{160,128},{192,160},{224,192},{256... | collective-permute-start | bytes 884744 | tf_op jit(solution)/shard_map/while/body/eval_jaxpr/ppermute | solution.py:12
  219.8 52.1 %all-reduce.2.cloned.1.call-done = f32[384,384]{1,0:T(8,128)} async-done(((f32[384,384]{1,0:T(8,128)}), f32[384,384]{1,0:T(8,128)}) %all-reduce.2.cloned.1.call-update) | async-done | bytes 589840 | tf_op jit(solution)/shard_map/psum | solution.py:68
  277.7 6.2 %collective-permute-done.12 = bf16[384,384]{1,0:T(8,128)(2,1)S(1)} collective-permute-done((bf16[384,384]{1,0:T(8,128)(2,1)S(1)}, bf16[384,384]{1,0:T(8,128)(2,1)S(1)}, u32[]{:S(2)}, u32[]{:S(2)}) %collective-permute-start.12) | collective-permute-done | bytes 294944 | tf_op jit(solution)/shard_map/ppermute | solution.py:12
  288.9 8.6 %collective-permute-done.13 = bf16[384,384]{1,0:T(8,128)(2,1)S(1)} collective-permute-done((bf16[384,384]{1,0:T(8,128)(2,1)S(1)}, bf16[384,384]{1,0:T(8,128)(2,1)S(1)}, u32[]{:S(2)}, u32[]{:S(2)}) %collective-permute-start.13) | collective-permute-done | bytes 294944 | tf_op jit(solution)/shard_map/ppermute | solution.py:12
  297.5 7.5 %collective-permute-start.14 = (bf16[384,384]{1,0:T(8,128)(2,1)S(1)}, bf16[384,384]{1,0:T(8,128)(2,1)S(1)}, u32[]{:S(2)}, u32[]{:S(2)}) collective-permute-start(bf16[384,384]{1,0:T(8,128)(2,1)S(1)} %broadcast_select_fusion.6), channel_id=1, source_target_pairs={{8,0},{10,2},{12,4},{14,6},{16,8},{18,10},{20,12},{22,14},{24,16},... | collective-permute-start | bytes 884744 | tf_op jit(solution)/shard_map/ppermute | solution.py:12
  305.0 18.5 %collective-permute-done.14 = bf16[384,384]{1,0:T(8,128)(2,1)S(1)} collective-permute-done((bf16[384,384]{1,0:T(8,128)(2,1)S(1)}, bf16[384,384]{1,0:T(8,128)(2,1)S(1)}, u32[]{:S(2)}, u32[]{:S(2)}) %collective-permute-start.14) | collective-permute-done | bytes 294944 | tf_op jit(solution)/shard_map/ppermute | solution.py:12
  323.6 11.8 %collective-permute-start.15 = (bf16[384,384]{1,0:T(8,128)(2,1)S(1)}, bf16[384,384]{1,0:T(8,128)(2,1)S(1)}, u32[]{:S(2)}, u32[]{:S(2)}) collective-permute-start(bf16[384,384]{1,0:T(8,128)(2,1)S(1)} %broadcast_select_fusion.8), channel_id=1, source_target_pairs={{16,0},{18,2},{20,4},{22,6},{24,8},{26,10},{28,12},{30,14},{0,16},... | collective-permute-start | bytes 884744 | tf_op jit(solution)/shard_map/ppermute | solution.py:12
  335.5 19.5 %collective-permute-done.15 = bf16[384,384]{1,0:T(8,128)(2,1)S(1)} collective-permute-done((bf16[384,384]{1,0:T(8,128)(2,1)S(1)}, bf16[384,384]{1,0:T(8,128)(2,1)S(1)}, u32[]{:S(2)}, u32[]{:S(2)}) %collective-permute-start.15) | collective-permute-done | bytes 294944 | tf_op jit(solution)/shard_map/ppermute | solution.py:12
  355.3 107.8 %while.29 = (s32[]{:T(128)}, f32[384,384]{1,0:T(8,128)S(1)}, bf16[384,384]{1,0:T(8,128)(2,1)S(1)}, bf16[384,384]{1,0:T(8,128)(2,1)S(1)}, s32[]{:T(128)}) while((s32[]{:T(128)}, f32[384,384]{1,0:T(8,128)S(1)}, bf16[384,384]{1,0:T(8,128)(2,1)S(1)}, bf16[384,384]{1,0:T(8,128)(2,1)S(1)}, s32[]{:T(128)}) %tuple.35), condition=%wide.region_4.5_spmd, body=%wide.region_3.4_spmd.sunk | while | flops 113393664 | bytes 5308557 | solution.py:51
  355.3 14.5 %collective-permute-start.2 = (bf16[384,384]{1,0:T(8,128)(2,1)S(1)}, bf16[384,384]{1,0:T(8,128)(2,1)S(1)}, u32[]{:S(2)}, u32[]{:S(2)}) collective-permute-start(bf16[384,384]{1,0:T(8,128)(2,1)S(1)} %get-tuple-element.141), channel_id=1, source_target_pairs={{2,0},{4,2},{6,4},{8,6},{10,8},{12,10},{14,12},{16,14},{18,16},{20... | collective-permute-start | bytes 884744 | tf_op jit(solution)/shard_map/while/body/eval_jaxpr/ppermute | solution.py:12
  369.8 6.5 %collective-permute-start.3 = (bf16[384,384]{1,0:T(8,128)(2,1)S(1)}, bf16[384,384]{1,0:T(8,128)(2,1)S(1)}, u32[]{:S(2)}, u32[]{:S(2)}) collective-permute-start(bf16[384,384]{1,0:T(8,128)(2,1)S(1)} %get-tuple-element.142), channel_id=1, source_target_pairs={{32,0},{64,32},{96,64},{128,96},{160,128},{192,160},{224,192},{256... | collective-permute-start | bytes 884744 | tf_op jit(solution)/shard_map/while/body/eval_jaxpr/ppermute | solution.py:12
  384.2 7.4 %collective-permute-start.3 = (bf16[384,384]{1,0:T(8,128)(2,1)S(1)}, bf16[384,384]{1,0:T(8,128)(2,1)S(1)}, u32[]{:S(2)}, u32[]{:S(2)}) collective-permute-start(bf16[384,384]{1,0:T(8,128)(2,1)S(1)} %get-tuple-element.142), channel_id=1, source_target_pairs={{32,0},{64,32},{96,64},{128,96},{160,128},{192,160},{224,192},{256... | collective-permute-start | bytes 884744 | tf_op jit(solution)/shard_map/while/body/eval_jaxpr/ppermute | solution.py:12
  398.6 7.4 %collective-permute-start.3 = (bf16[384,384]{1,0:T(8,128)(2,1)S(1)}, bf16[384,384]{1,0:T(8,128)(2,1)S(1)}, u32[]{:S(2)}, u32[]{:S(2)}) collective-permute-start(bf16[384,384]{1,0:T(8,128)(2,1)S(1)} %get-tuple-element.142), channel_id=1, source_target_pairs={{32,0},{64,32},{96,64},{128,96},{160,128},{192,160},{224,192},{256... | collective-permute-start | bytes 884744 | tf_op jit(solution)/shard_map/while/body/eval_jaxpr/ppermute | solution.py:12
  412.1 7.5 %collective-permute-start.3 = (bf16[384,384]{1,0:T(8,128)(2,1)S(1)}, bf16[384,384]{1,0:T(8,128)(2,1)S(1)}, u32[]{:S(2)}, u32[]{:S(2)}) collective-permute-start(bf16[384,384]{1,0:T(8,128)(2,1)S(1)} %get-tuple-element.142), channel_id=1, source_target_pairs={{32,0},{64,32},{96,64},{128,96},{160,128},{192,160},{224,192},{256... | collective-permute-start | bytes 884744 | tf_op jit(solution)/shard_map/while/body/eval_jaxpr/ppermute | solution.py:12
  425.5 7.1 %collective-permute-start.3 = (bf16[384,384]{1,0:T(8,128)(2,1)S(1)}, bf16[384,384]{1,0:T(8,128)(2,1)S(1)}, u32[]{:S(2)}, u32[]{:S(2)}) collective-permute-start(bf16[384,384]{1,0:T(8,128)(2,1)S(1)} %get-tuple-element.142), channel_id=1, source_target_pairs={{32,0},{64,32},{96,64},{128,96},{160,128},{192,160},{224,192},{256... | collective-permute-start | bytes 884744 | tf_op jit(solution)/shard_map/while/body/eval_jaxpr/ppermute | solution.py:12
  438.7 7.1 %collective-permute-start.3 = (bf16[384,384]{1,0:T(8,128)(2,1)S(1)}, bf16[384,384]{1,0:T(8,128)(2,1)S(1)}, u32[]{:S(2)}, u32[]{:S(2)}) collective-permute-start(bf16[384,384]{1,0:T(8,128)(2,1)S(1)} %get-tuple-element.142), channel_id=1, source_target_pairs={{32,0},{64,32},{96,64},{128,96},{160,128},{192,160},{224,192},{256... | collective-permute-start | bytes 884744 | tf_op jit(solution)/shard_map/while/body/eval_jaxpr/ppermute | solution.py:12
  451.9 7.1 %collective-permute-start.3 = (bf16[384,384]{1,0:T(8,128)(2,1)S(1)}, bf16[384,384]{1,0:T(8,128)(2,1)S(1)}, u32[]{:S(2)}, u32[]{:S(2)}) collective-permute-start(bf16[384,384]{1,0:T(8,128)(2,1)S(1)} %get-tuple-element.142), channel_id=1, source_target_pairs={{32,0},{64,32},{96,64},{128,96},{160,128},{192,160},{224,192},{256... | collective-permute-start | bytes 884744 | tf_op jit(solution)/shard_map/while/body/eval_jaxpr/ppermute | solution.py:12
  464.2 27.5 %reduce-scatter.2.cloned.1.call-done = f32[192,384]{1,0:T(8,128)} async-done(((f32[384,384]{1,0:T(8,128)}), f32[192,384]{1,0:T(8,128)}) %reduce-scatter.2.cloned.1.call-update) | async-done | bytes 294928 | tf_op jit(solution)/shard_map/reduce_scatter | solution.py:71
  (126 shorter events, 131.1 us)
Async XLA Ops:
  6.5 265.4 %all-reduce.2.cloned.1.call-start = ((), (), s32[]{:S(2)}) async-start(), calls=%async_computation.1 | async-start | bytes 1179648 | tf_op jit(solution)/shard_map/psum | solution.py:68
  6.5 18.8 %collective-permute-start.4 = (bf16[384,384]{1,0:T(8,128)(2,1)}, bf16[384,384]{1,0:T(8,128)(2,1)S(1)}, u32[]{:S(2)}, u32[]{:S(2)}) collective-permute-start(bf16[384,384]{1,0:T(8,128)(2,1)} %param.6), channel_id=1, source_target_pairs={{2,0},{4,2},{6,4},{8,6},{10,8},{12,10},{14,12},{16,14},{18,16},{20... | collective-permute-start | bytes 884744 | tf_op jit(solution)/shard_map/ppermute | solution.py:12
  18.5 12.5 %collective-permute-start.8 = (bf16[384,384]{1,0:T(8,128)(2,1)}, bf16[384,384]{1,0:T(8,128)(2,1)S(1)}, u32[]{:S(2)}, u32[]{:S(2)}) collective-permute-start(bf16[384,384]{1,0:T(8,128)(2,1)} %param.6), channel_id=1, source_target_pairs={{32,0},{64,32},{96,64},{128,96},{160,128},{192,160},{224,192},{256... | collective-permute-start | bytes 884744 | tf_op jit(solution)/shard_map/ppermute | solution.py:12
  32.0 10.0 %collective-permute-start.9 = (bf16[384,384]{1,0:T(8,128)(2,1)S(1)}, bf16[384,384]{1,0:T(8,128)(2,1)S(1)}, u32[]{:S(2)}, u32[]{:S(2)}) collective-permute-start(bf16[384,384]{1,0:T(8,128)(2,1)S(1)} %get-tuple-element.67), channel_id=1, source_target_pairs={{64,0},{96,32},{128,64},{160,96},{192,128},{224,160},{256,192},{28... | collective-permute-start | bytes 884744 | tf_op jit(solution)/shard_map/ppermute | solution.py:12
  36.2 13.6 %collective-permute-start.5 = (bf16[384,384]{1,0:T(8,128)(2,1)S(1)}, bf16[384,384]{1,0:T(8,128)(2,1)S(1)}, u32[]{:S(2)}, u32[]{:S(2)}) collective-permute-start(bf16[384,384]{1,0:T(8,128)(2,1)S(1)} %get-tuple-element.68), channel_id=1, source_target_pairs={{4,0},{6,2},{8,4},{10,6},{12,8},{14,10},{16,12},{18,14},{20,16},{2... | collective-permute-start | bytes 884744 | tf_op jit(solution)/shard_map/ppermute | solution.py:12
  42.1 14.2 %collective-permute-start.10 = (bf16[384,384]{1,0:T(8,128)(2,1)S(1)}, bf16[384,384]{1,0:T(8,128)(2,1)S(1)}, u32[]{:S(2)}, u32[]{:S(2)}) collective-permute-start(bf16[384,384]{1,0:T(8,128)(2,1)S(1)} %broadcast_select_fusion.1), channel_id=1, source_target_pairs={{128,0},{160,32},{192,64},{224,96},{256,128},{288,160},{320,192},{... | collective-permute-start | bytes 884744 | tf_op jit(solution)/shard_map/ppermute | solution.py:12
  49.9 20.3 %collective-permute-start.6 = (bf16[384,384]{1,0:T(8,128)(2,1)S(1)}, bf16[384,384]{1,0:T(8,128)(2,1)S(1)}, u32[]{:S(2)}, u32[]{:S(2)}) collective-permute-start(bf16[384,384]{1,0:T(8,128)(2,1)S(1)} %broadcast_select_fusion.7), channel_id=1, source_target_pairs={{8,0},{10,2},{12,4},{14,6},{16,8},{18,10},{20,12},{22,14},{24,16},... | collective-permute-start | bytes 884744 | tf_op jit(solution)/shard_map/ppermute | solution.py:12
  56.3 18.4 %collective-permute-start.11 = (bf16[384,384]{1,0:T(8,128)(2,1)S(1)}, bf16[384,384]{1,0:T(8,128)(2,1)S(1)}, u32[]{:S(2)}, u32[]{:S(2)}) collective-permute-start(bf16[384,384]{1,0:T(8,128)(2,1)S(1)} %broadcast_select_fusion.2), channel_id=1, source_target_pairs={{256,0},{288,32},{320,64},{352,96},{384,128},{416,160},{448,192},{... | collective-permute-start | bytes 884744 | tf_op jit(solution)/shard_map/ppermute | solution.py:12
  70.2 25.0 %collective-permute-start.7 = (bf16[384,384]{1,0:T(8,128)(2,1)S(1)}, bf16[384,384]{1,0:T(8,128)(2,1)S(1)}, u32[]{:S(2)}, u32[]{:S(2)}) collective-permute-start(bf16[384,384]{1,0:T(8,128)(2,1)S(1)} %broadcast_select_fusion.9), channel_id=1, source_target_pairs={{16,0},{18,2},{20,4},{22,6},{24,8},{26,10},{28,12},{30,14},{0,16},... | collective-permute-start | bytes 884744 | tf_op jit(solution)/shard_map/ppermute | solution.py:12
  95.7 29.0 %collective-permute-start = (bf16[384,384]{1,0:T(8,128)(2,1)S(1)}, bf16[384,384]{1,0:T(8,128)(2,1)S(1)}, u32[]{:S(2)}, u32[]{:S(2)}) collective-permute-start(bf16[384,384]{1,0:T(8,128)(2,1)S(1)} %get-tuple-element.126), channel_id=1, source_target_pairs={{2,0},{4,2},{6,4},{8,6},{10,8},{12,10},{14,12},{16,14},{18,16},{20... | collective-permute-start | bytes 884744 | tf_op jit(solution)/shard_map/while/body/eval_jaxpr/ppermute | solution.py:12
  119.2 11.8 %collective-permute-start.1 = (bf16[384,384]{1,0:T(8,128)(2,1)S(1)}, bf16[384,384]{1,0:T(8,128)(2,1)S(1)}, u32[]{:S(2)}, u32[]{:S(2)}) collective-permute-start(bf16[384,384]{1,0:T(8,128)(2,1)S(1)} %get-tuple-element.127), channel_id=1, source_target_pairs={{32,0},{64,32},{96,64},{128,96},{160,128},{192,160},{224,192},{256... | collective-permute-start | bytes 884744 | tf_op jit(solution)/shard_map/while/body/eval_jaxpr/ppermute | solution.py:12
  144.9 11.1 %collective-permute-start.1 = (bf16[384,384]{1,0:T(8,128)(2,1)S(1)}, bf16[384,384]{1,0:T(8,128)(2,1)S(1)}, u32[]{:S(2)}, u32[]{:S(2)}) collective-permute-start(bf16[384,384]{1,0:T(8,128)(2,1)S(1)} %get-tuple-element.127), channel_id=1, source_target_pairs={{32,0},{64,32},{96,64},{128,96},{160,128},{192,160},{224,192},{256... | collective-permute-start | bytes 884744 | tf_op jit(solution)/shard_map/while/body/eval_jaxpr/ppermute | solution.py:12
  158.4 11.3 %collective-permute-start.1 = (bf16[384,384]{1,0:T(8,128)(2,1)S(1)}, bf16[384,384]{1,0:T(8,128)(2,1)S(1)}, u32[]{:S(2)}, u32[]{:S(2)}) collective-permute-start(bf16[384,384]{1,0:T(8,128)(2,1)S(1)} %get-tuple-element.127), channel_id=1, source_target_pairs={{32,0},{64,32},{96,64},{128,96},{160,128},{192,160},{224,192},{256... | collective-permute-start | bytes 884744 | tf_op jit(solution)/shard_map/while/body/eval_jaxpr/ppermute | solution.py:12
  170.1 16.9 %collective-permute-start = (bf16[384,384]{1,0:T(8,128)(2,1)S(1)}, bf16[384,384]{1,0:T(8,128)(2,1)S(1)}, u32[]{:S(2)}, u32[]{:S(2)}) collective-permute-start(bf16[384,384]{1,0:T(8,128)(2,1)S(1)} %get-tuple-element.126), channel_id=1, source_target_pairs={{2,0},{4,2},{6,4},{8,6},{10,8},{12,10},{14,12},{16,14},{18,16},{20... | collective-permute-start | bytes 884744 | tf_op jit(solution)/shard_map/while/body/eval_jaxpr/ppermute | solution.py:12
  179.8 10.8 %collective-permute-start.1 = (bf16[384,384]{1,0:T(8,128)(2,1)S(1)}, bf16[384,384]{1,0:T(8,128)(2,1)S(1)}, u32[]{:S(2)}, u32[]{:S(2)}) collective-permute-start(bf16[384,384]{1,0:T(8,128)(2,1)S(1)} %get-tuple-element.127), channel_id=1, source_target_pairs={{32,0},{64,32},{96,64},{128,96},{160,128},{192,160},{224,192},{256... | collective-permute-start | bytes 884744 | tf_op jit(solution)/shard_map/while/body/eval_jaxpr/ppermute | solution.py:12
  191.1 9.7 %collective-permute-start = (bf16[384,384]{1,0:T(8,128)(2,1)S(1)}, bf16[384,384]{1,0:T(8,128)(2,1)S(1)}, u32[]{:S(2)}, u32[]{:S(2)}) collective-permute-start(bf16[384,384]{1,0:T(8,128)(2,1)S(1)} %get-tuple-element.126), channel_id=1, source_target_pairs={{2,0},{4,2},{6,4},{8,6},{10,8},{12,10},{14,12},{16,14},{18,16},{20... | collective-permute-start | bytes 884744 | tf_op jit(solution)/shard_map/while/body/eval_jaxpr/ppermute | solution.py:12
  193.6 10.8 %collective-permute-start.1 = (bf16[384,384]{1,0:T(8,128)(2,1)S(1)}, bf16[384,384]{1,0:T(8,128)(2,1)S(1)}, u32[]{:S(2)}, u32[]{:S(2)}) collective-permute-start(bf16[384,384]{1,0:T(8,128)(2,1)S(1)} %get-tuple-element.127), channel_id=1, source_target_pairs={{32,0},{64,32},{96,64},{128,96},{160,128},{192,160},{224,192},{256... | collective-permute-start | bytes 884744 | tf_op jit(solution)/shard_map/while/body/eval_jaxpr/ppermute | solution.py:12
  207.1 10.8 %collective-permute-start.1 = (bf16[384,384]{1,0:T(8,128)(2,1)S(1)}, bf16[384,384]{1,0:T(8,128)(2,1)S(1)}, u32[]{:S(2)}, u32[]{:S(2)}) collective-permute-start(bf16[384,384]{1,0:T(8,128)(2,1)S(1)} %get-tuple-element.127), channel_id=1, source_target_pairs={{32,0},{64,32},{96,64},{128,96},{160,128},{192,160},{224,192},{256... | collective-permute-start | bytes 884744 | tf_op jit(solution)/shard_map/while/body/eval_jaxpr/ppermute | solution.py:12
  219.2 272.6 %reduce-scatter.2.cloned.1.call-start = ((), (), s32[]{:S(2)}) async-start(), calls=%async_computation.2 | async-start | bytes 884736 | tf_op jit(solution)/shard_map/reduce_scatter | solution.py:71
  273.0 10.8 %collective-permute-start.12 = (bf16[384,384]{1,0:T(8,128)(2,1)S(1)}, bf16[384,384]{1,0:T(8,128)(2,1)S(1)}, u32[]{:S(2)}, u32[]{:S(2)}) collective-permute-start(bf16[384,384]{1,0:T(8,128)(2,1)S(1)} %multiply_convert_fusion), channel_id=1, source_target_pairs={{2,0},{4,2},{6,4},{8,6},{10,8},{12,10},{14,12},{16,14},{18,16},{20... | collective-permute-start | bytes 884744 | tf_op jit(solution)/shard_map/ppermute | solution.py:12
  283.9 13.5 %collective-permute-start.13 = (bf16[384,384]{1,0:T(8,128)(2,1)S(1)}, bf16[384,384]{1,0:T(8,128)(2,1)S(1)}, u32[]{:S(2)}, u32[]{:S(2)}) collective-permute-start(bf16[384,384]{1,0:T(8,128)(2,1)S(1)} %broadcast_select_fusion.4), channel_id=1, source_target_pairs={{4,0},{6,2},{8,4},{10,6},{12,8},{14,10},{16,12},{18,14},{20,16},{2... | collective-permute-start | bytes 884744 | tf_op jit(solution)/shard_map/ppermute | solution.py:12
  297.5 26.1 %collective-permute-start.14 = (bf16[384,384]{1,0:T(8,128)(2,1)S(1)}, bf16[384,384]{1,0:T(8,128)(2,1)S(1)}, u32[]{:S(2)}, u32[]{:S(2)}) collective-permute-start(bf16[384,384]{1,0:T(8,128)(2,1)S(1)} %broadcast_select_fusion.6), channel_id=1, source_target_pairs={{8,0},{10,2},{12,4},{14,6},{16,8},{18,10},{20,12},{22,14},{24,16},... | collective-permute-start | bytes 884744 | tf_op jit(solution)/shard_map/ppermute | solution.py:12
  323.6 31.3 %collective-permute-start.15 = (bf16[384,384]{1,0:T(8,128)(2,1)S(1)}, bf16[384,384]{1,0:T(8,128)(2,1)S(1)}, u32[]{:S(2)}, u32[]{:S(2)}) collective-permute-start(bf16[384,384]{1,0:T(8,128)(2,1)S(1)} %broadcast_select_fusion.8), channel_id=1, source_target_pairs={{16,0},{18,2},{20,4},{22,6},{24,8},{26,10},{28,12},{30,14},{0,16},... | collective-permute-start | bytes 884744 | tf_op jit(solution)/shard_map/ppermute | solution.py:12
  355.3 21.0 %collective-permute-start.2 = (bf16[384,384]{1,0:T(8,128)(2,1)S(1)}, bf16[384,384]{1,0:T(8,128)(2,1)S(1)}, u32[]{:S(2)}, u32[]{:S(2)}) collective-permute-start(bf16[384,384]{1,0:T(8,128)(2,1)S(1)} %get-tuple-element.141), channel_id=1, source_target_pairs={{2,0},{4,2},{6,4},{8,6},{10,8},{12,10},{14,12},{16,14},{18,16},{20... | collective-permute-start | bytes 884744 | tf_op jit(solution)/shard_map/while/body/eval_jaxpr/ppermute | solution.py:12
  369.8 11.7 %collective-permute-start.3 = (bf16[384,384]{1,0:T(8,128)(2,1)S(1)}, bf16[384,384]{1,0:T(8,128)(2,1)S(1)}, u32[]{:S(2)}, u32[]{:S(2)}) collective-permute-start(bf16[384,384]{1,0:T(8,128)(2,1)S(1)} %get-tuple-element.142), channel_id=1, source_target_pairs={{32,0},{64,32},{96,64},{128,96},{160,128},{192,160},{224,192},{256... | collective-permute-start | bytes 884744 | tf_op jit(solution)/shard_map/while/body/eval_jaxpr/ppermute | solution.py:12
  382.0 9.7 %collective-permute-start.2 = (bf16[384,384]{1,0:T(8,128)(2,1)S(1)}, bf16[384,384]{1,0:T(8,128)(2,1)S(1)}, u32[]{:S(2)}, u32[]{:S(2)}) collective-permute-start(bf16[384,384]{1,0:T(8,128)(2,1)S(1)} %get-tuple-element.141), channel_id=1, source_target_pairs={{2,0},{4,2},{6,4},{8,6},{10,8},{12,10},{14,12},{16,14},{18,16},{20... | collective-permute-start | bytes 884744 | tf_op jit(solution)/shard_map/while/body/eval_jaxpr/ppermute | solution.py:12
  384.2 11.8 %collective-permute-start.3 = (bf16[384,384]{1,0:T(8,128)(2,1)S(1)}, bf16[384,384]{1,0:T(8,128)(2,1)S(1)}, u32[]{:S(2)}, u32[]{:S(2)}) collective-permute-start(bf16[384,384]{1,0:T(8,128)(2,1)S(1)} %get-tuple-element.142), channel_id=1, source_target_pairs={{32,0},{64,32},{96,64},{128,96},{160,128},{192,160},{224,192},{256... | collective-permute-start | bytes 884744 | tf_op jit(solution)/shard_map/while/body/eval_jaxpr/ppermute | solution.py:12
  398.6 11.1 %collective-permute-start.3 = (bf16[384,384]{1,0:T(8,128)(2,1)S(1)}, bf16[384,384]{1,0:T(8,128)(2,1)S(1)}, u32[]{:S(2)}, u32[]{:S(2)}) collective-permute-start(bf16[384,384]{1,0:T(8,128)(2,1)S(1)} %get-tuple-element.142), channel_id=1, source_target_pairs={{32,0},{64,32},{96,64},{128,96},{160,128},{192,160},{224,192},{256... | collective-permute-start | bytes 884744 | tf_op jit(solution)/shard_map/while/body/eval_jaxpr/ppermute | solution.py:12
  412.1 11.1 %collective-permute-start.3 = (bf16[384,384]{1,0:T(8,128)(2,1)S(1)}, bf16[384,384]{1,0:T(8,128)(2,1)S(1)}, u32[]{:S(2)}, u32[]{:S(2)}) collective-permute-start(bf16[384,384]{1,0:T(8,128)(2,1)S(1)} %get-tuple-element.142), channel_id=1, source_target_pairs={{32,0},{64,32},{96,64},{128,96},{160,128},{192,160},{224,192},{256... | collective-permute-start | bytes 884744 | tf_op jit(solution)/shard_map/while/body/eval_jaxpr/ppermute | solution.py:12
  425.5 10.8 %collective-permute-start.3 = (bf16[384,384]{1,0:T(8,128)(2,1)S(1)}, bf16[384,384]{1,0:T(8,128)(2,1)S(1)}, u32[]{:S(2)}, u32[]{:S(2)}) collective-permute-start(bf16[384,384]{1,0:T(8,128)(2,1)S(1)} %get-tuple-element.142), channel_id=1, source_target_pairs={{32,0},{64,32},{96,64},{128,96},{160,128},{192,160},{224,192},{256... | collective-permute-start | bytes 884744 | tf_op jit(solution)/shard_map/while/body/eval_jaxpr/ppermute | solution.py:12
  438.7 10.8 %collective-permute-start.3 = (bf16[384,384]{1,0:T(8,128)(2,1)S(1)}, bf16[384,384]{1,0:T(8,128)(2,1)S(1)}, u32[]{:S(2)}, u32[]{:S(2)}) collective-permute-start(bf16[384,384]{1,0:T(8,128)(2,1)S(1)} %get-tuple-element.142), channel_id=1, source_target_pairs={{32,0},{64,32},{96,64},{128,96},{160,128},{192,160},{224,192},{256... | collective-permute-start | bytes 884744 | tf_op jit(solution)/shard_map/while/body/eval_jaxpr/ppermute | solution.py:12
  451.9 10.8 %collective-permute-start.3 = (bf16[384,384]{1,0:T(8,128)(2,1)S(1)}, bf16[384,384]{1,0:T(8,128)(2,1)S(1)}, u32[]{:S(2)}, u32[]{:S(2)}) collective-permute-start(bf16[384,384]{1,0:T(8,128)(2,1)S(1)} %get-tuple-element.142), channel_id=1, source_target_pairs={{32,0},{64,32},{96,64},{128,96},{160,128},{192,160},{224,192},{256... | collective-permute-start | bytes 884744 | tf_op jit(solution)/shard_map/while/body/eval_jaxpr/ppermute | solution.py:12
  (13 other events, 216.7 us)
Sparse Core Ops, SparseCore 0:
  219.3 52.5 all-reduce.1
  464.0 27.6 reduce-scatter.1
where the time goes:
time: 502 us; the launch traced here: 500 us
  waiting for transfers between devices  238 us (47%)
  starting transfers between devices  234 us (47%)
  between operations  13.7 us (3%)
  matrix products  6.04 us (1%)
    ppermute x40, starting transfers between devices, passed_along(): return lax.ppermute(block, axis, route)  234 us
    ppermute x40, waiting for transfers between devices, passed_along(): return lax.ppermute(block, axis, route)  158 us
    psum x1, waiting for transfers between devices, shards(): summed = lax.psum(partial_value, 'layer')  52.1 us
    reduce_scatter x1, waiting for transfers between devices, shards(): lax.psum_scatter(partial_value, 'layer', scatter_dimension=0, tiled=True)  27.5 us
  transfers between devices with their start and end apart: 42, of which 27 were waited for; matrix products, arithmetic and copies ran while one was open for 0% of the time, Pallas kernels for 0%

commit v1 on v0

v1 whole, which is shorter than its diff:
```python
import jax
import jax.numpy as jnp
from jax import lax
from jax.sharding import PartitionSpec as P

TILE = 64


def expand_tiles(tile_mask):
    tile_rows, tile_cols = tile_mask.shape
    tile_grid = tile_mask.astype(jnp.float32)[:, None, :, None]
    return jnp.broadcast_to(tile_grid, (tile_rows, TILE, tile_cols, TILE)).reshape(
        tile_rows * TILE, tile_cols * TILE
    )


def strip_product(left_blocks, right_blocks):
    total = jnp.dot(left_blocks[0], right_blocks[0], preferred_element_type=jnp.float32)
    for k in range(1, left_blocks.shape[0]):
        total += jnp.dot(left_blocks[k], right_blocks[k], preferred_element_type=jnp.float32)
    return total


def shards(density, product_pattern):
    layers = lax.axis_size("layer")
    layer_pos = lax.axis_index("layer")
    half_rows = density.shape[0] // layers
    mask_rows = lax.dynamic_slice_in_dim(
        product_pattern, layer_pos * (half_rows // TILE), half_rows // TILE, 0
    )
    mask = expand_tiles(mask_rows)
    mine = lax.dynamic_slice_in_dim(density, layer_pos * half_rows, half_rows, 0)
    left = lax.all_gather(mine, "col")
    right = lax.all_gather(density, "row")
    squared = (strip_product(left, right) * mask).astype(jnp.bfloat16)
    left = lax.all_gather(squared, "col")
    cubed = strip_product(left, right)
    result = (3.0 * squared.astype(jnp.float32) - 2.0 * cubed) * mask
    return result.astype(jnp.bfloat16)


def solution(mesh):
    placed = (P("row", "col"), P("row", "col"))
    return jax.shard_map(
        shards, mesh=mesh, in_specs=placed, out_specs=P(("row", "layer"), "col"), check_vma=False
    )
```

time: 502 us -> 272 us (0.54)
  the two profiles are of different devices: /device:TPU:1 before, /device:TPU:8 now
where the time goes in v1:
time: 272 us; the launch traced here: 271 us
  waiting for transfers between devices  222 us (82%)
  matrix products  33.1 us (12%)
  between operations  13.4 us (5%)
    all_gather x1, waiting for transfers between devices, shards(): left = lax.all_gather(mine, 'col')  78.2 us
    all_gather x1, waiting for transfers between devices, shards(): left = lax.all_gather(squared, 'col')  74.3 us
    all_gather x1, waiting for transfers between devices, shards(): right = lax.all_gather(density, 'row')  69 us
    dot_general x30, matrix products, strip_product(): jnp.dot(left_blocks[k], right_blocks[k], preferred_element_type=jnp.float32)  30.3 us
  transfers between devices with their start and end apart: 3, of which 3 were waited for; matrix products, arithmetic and copies ran while one was open for 0% of the time, Pallas kernels for 0%

profile of v1, /device:TPU:8, one launch (start us, length us, event | category | flops | bytes accessed | tf_op | source)
XLA Modules:
  0.0 271.4 jit_solution(13455970528942908509)
XLA Ops:
  6.5 1.6 constant_dynamic-slice_fusion
  8.2 0.7 all-gather.9.cloned.1.call-update
  8.9 0.7 dynamic-slice_convert_fusion
  9.9 78.2 %all-gather.7.cloned.1.call-done = bf16[3072,384]{1,0:T(8,128)(2,1)} async-done(((bf16[192,384]{1,0:T(8,128)(2,1)}), bf16[3072,384]{1,0:T(8,128)(2,1)}) %all-gather.7.cloned.1.call-update) | async-done | bytes 2359312 | tf_op jit(solution)/shard_map/all_gather | solution.py:33
  88.2 69.0 %all-gather.9.cloned.1.call-done = bf16[6144,384]{1,0:T(8,128)(2,1)} async-done(((bf16[384,384]{1,0:T(8,128)(2,1)}), bf16[6144,384]{1,0:T(8,128)(2,1)}) %all-gather.9.cloned.1.call-update) | async-done | bytes 4718608 | tf_op jit(solution)/shard_map/all_gather | solution.py:34
  157.1 1.4 fusion.36
  158.6 1.4 convolution_add_fusion.29
  160.0 1.3 convolution_add_fusion.28
  161.3 1.4 convolution_add_fusion.27
  162.7 1.3 convolution_add_fusion.26
  164.0 1.1 convolution_add_fusion.25
  165.2 1.1 convolution_add_fusion.24
  166.3 1.1 convolution_add_fusion.23
  168.9 0.2 convolution_add_fusion.16
  169.2 0.9 fusion.4
  170.1 74.3 %all-gather.11.cloned.1.call-done = bf16[3072,384]{1,0:T(8,128)(2,1)} async-done(((bf16[192,384]{1,0:T(8,128)(2,1)}), bf16[3072,384]{1,0:T(8,128)(2,1)}) %all-gather.11.cloned.1.call-update) | async-done | bytes 2359312 | tf_op jit(solution)/shard_map/all_gather | solution.py:36
  244.4 1.4 fusion.38
  245.9 1.3 convolution_add_fusion.14
  247.1 1.3 convolution_add_fusion.13
  248.4 1.2 convolution_add_fusion.12
  249.6 1.2 convolution_add_fusion.11
  250.8 1.2 convolution_add_fusion.10
  252.1 1.2 convolution_add_fusion.9
  253.3 1.2 convolution_add_fusion.8
  254.5 1.2 convolution_add_fusion.7
  255.7 1.2 convolution_add_fusion.6
  256.9 1.2 convolution_add_fusion.5
  258.1 1.2 convolution_add_fusion.4
  259.3 1.2 convolution_add_fusion.3
  260.6 1.2 convolution_add_fusion.2
  261.8 1.2 convolution_add_fusion.1
  263.0 1.9 fusion.5
  (21 shorter events, 1.8 us)
Async XLA Ops:
  6.5 81.6 %all-gather.7.cloned.1.call-start = ((), (), s32[]{:S(2)}) async-start(), calls=%async_computation | async-start | bytes 2506752 | tf_op jit(solution)/shard_map/all_gather | solution.py:33
  8.1 149.0 %all-gather.9.cloned.1.call-start = ((), (), s32[]{:S(2)}) async-start(), calls=%async_computation.1 | async-start | bytes 5013504 | tf_op jit(solution)/shard_map/all_gather | solution.py:34
  8.9 235.5 %all-gather.11.cloned.1.call-start = ((), (), s32[]{:S(2)}) async-start(), calls=%async_computation.2 | async-start | bytes 2506752 | tf_op jit(solution)/shard_map/all_gather | solution.py:36
  157.1 6.9 %copy-start = (bf16[6144,384]{1,0:T(8,128)(2,1)S(1)}, bf16[6144,384]{1,0:T(8,128)(2,1)}, u32[]{:S(2)}) copy-start(bf16[6144,384]{1,0:T(8,128)(2,1)} %all-gather.9.cloned.1.call-done) | copy-start | bytes 14155780
  161.3 6.2 %copy-start.1 = (bf16[3072,384]{1,0:T(8,128)(2,1)S(1)}, bf16[3072,384]{1,0:T(8,128)(2,1)}, u32[]{:S(2)}) copy-start(bf16[3072,384]{1,0:T(8,128)(2,1)} %all-gather.7.cloned.1.call-done) | copy-start | bytes 7077892
  244.4 4.0 %copy-start.2 = (bf16[3072,384]{1,0:T(8,128)(2,1)S(1)}, bf16[3072,384]{1,0:T(8,128)(2,1)}, u32[]{:S(2)}) copy-start(bf16[3072,384]{1,0:T(8,128)(2,1)} %all-gather.11.cloned.1.call-done) | copy-start | bytes 7077892
  256.9 6.1 %copy-start.3 = (bf16[192,384]{1,0:T(8,128)(2,1)S(1)}, bf16[192,384]{1,0:T(8,128)(2,1)}, u32[]{:S(2)}) copy-start(bf16[192,384]{1,0:T(8,128)(2,1)} %fusion.4) | copy-start | bytes 442372
Sparse Core Ops, SparseCore 0:
  9.4 78.6 all-gather.6
  91.2 65.8 all-gather.8
  170.2 74.1 all-gather.10

commit v2 on v1

v2 whole, which is shorter than its diff:
```python
import jax
import jax.numpy as jnp
from jax import lax
from jax.sharding import PartitionSpec as P

TILE = 64
TAIL = 8


def expand_tiles(tile_mask):
    tile_rows, tile_cols = tile_mask.shape
    tile_grid = tile_mask.astype(jnp.float32)[:, None, :, None]
    return jnp.broadcast_to(tile_grid, (tile_rows, TILE, tile_cols, TILE)).reshape(
        tile_rows * TILE, tile_cols * TILE
    )


def pack(block):
    block = block.astype(jnp.float32)
    largest = jnp.maximum(jnp.max(jnp.abs(block)), 1e-30)
    exponent = jnp.floor(jnp.log2(largest))
    scaled = (block * jnp.exp2(14.0 - exponent)).astype(jnp.float16)
    tail = jnp.full((TAIL, block.shape[1]), exponent).astype(jnp.float16)
    return jnp.concatenate([scaled, tail])


def unpack(packed):
    exponent = packed[:, -TAIL:-TAIL + 1, :1].astype(jnp.float32)
    return (packed[:, :-TAIL].astype(jnp.float32) * jnp.exp2(exponent - 14.0)).astype(jnp.bfloat16)


def shards(density, product_pattern):
    layers = lax.axis_size("layer")
    layer_pos = lax.axis_index("layer")
    rows = lax.axis_size("row")
    cols = lax.axis_size("col")
    side = density.shape[0]
    half = side // layers

    mine = lax.dynamic_slice_in_dim(density, layer_pos * half, half, 0)
    mine_t = lax.dynamic_slice_in_dim(density.T, layer_pos * half, half, 0)
    right = lax.all_to_all(jnp.broadcast_to(mine_t, (rows, half, side)), "row", 0, 0)
    left = lax.all_gather(pack(mine), ("col", "layer"))
    left = unpack(left).reshape(cols, side, side)
    other = lax.ppermute(right, "layer", [(i, layers - 1 - i) for i in range(layers)])

    mask = expand_tiles(product_pattern)
    mask_t = lax.dynamic_slice_in_dim(mask.T, layer_pos * half, half, 0)
    total = jnp.einsum("kjc,krc->jr", right, left, preferred_element_type=jnp.float32)
    squared_t = (total * mask_t).astype(jnp.bfloat16)
    strip = unpack(lax.all_gather(pack(squared_t), ("col", "layer"))).reshape(cols * side, side)
    strip = lax.dynamic_slice_in_dim(strip, layer_pos * half, half, 1).reshape(cols, side, half)

    low = jnp.where(layer_pos == 0, right, other)
    high = jnp.where(layer_pos == 0, other, right)
    cubed_t = jnp.concatenate(
        [
            jnp.einsum("kjc,kcr->jr", part, strip, preferred_element_type=jnp.float32)
            for part in (low, high)
        ]
    )
    square_t = lax.dynamic_index_in_dim(strip, lax.axis_index("col"), 0, keepdims=False)
    mask_rows = lax.dynamic_slice_in_dim(mask, layer_pos * half, half, 0)
    result = (3.0 * square_t.astype(jnp.float32) - 2.0 * cubed_t).T * mask_rows
    return result.astype(jnp.bfloat16)


def solution(mesh):
    placed = (P("row", "col"), P("row", "col"))
    return jax.shard_map(
        shards, mesh=mesh, in_specs=placed, out_specs=P(("row", "layer"), "col"), check_vma=False
    )
```

time: 272 us -> 142 us (0.52)
  the two profiles are of different devices: /device:TPU:8 before, /device:TPU:1 now
where the time goes in v2:
time: 142 us
  blocking collectives  97.3 us (69%)
  other arithmetic  11.5 us (8%)
  matrix products  11.2 us (8%)
  local copies, waits for them, and re-layouts  10.3 us (7%)
  starting transfers between devices  9.68 us (7%)
  between operations  1.69 us (1%)
    all_gather x1, blocking collectives, shards(): left = lax.all_gather(pack(mine), ('col', 'layer'))  52.9 us
    all_gather x1, blocking collectives, shards(): lax.all_gather(pack(squared_t), ('col', 'layer'))  44.4 us
    convert_element_type x2, other arithmetic, unpack(): (packed[:, :-TAIL].astype(jnp.float32) * jnp.exp2(exponent - 14.0)).astyp...  9.96 us
    all_to_all x1, starting transfers between devices, shards(): lax.all_to_all(jnp.broadcast_to(mine_t, (rows, half, side)), 'row', 0, 0)  7.63 us
    dot_general x2, matrix products, shards(): jnp.einsum('kjc,kcr->jr', part, strip, preferred_element_type=jnp.float32)  5.81 us
    dot_general x1, matrix products, shards(): jnp.einsum('kjc,krc->jr', right, left, preferred_element_type=jnp.float32)  5.34 us
    unnamed x16, local copies, waits for them, and re-layouts  4.88 us
  transfers between devices with their start and end apart: 2, of which 0 were waited for; matrix products, arithmetic and copies ran while one was open for 10% of the time, Pallas kernels for 0%

profile of v2, /device:TPU:1, one launch (start us, length us, event | category | flops | bytes accessed | tf_op | source)
XLA Modules:
  0.0 141.6 jit_solution(18254087242298644241)
XLA Ops:
  0.0 1.0 dynamic-slice_bitcast_fusion
  1.1 0.1 copy.43
  1.2 0.0 copy-start.4
  1.2 1.8 %broadcast_in_dim.4 = bf16[16,192,384]{2,1,0:T(8,128)(2,1)} broadcast(bf16[192,384]{1,0:T(8,128)(2,1)S(1)} %copy.43), dimensions={1,2} | broadcast | bytes 2506752 | tf_op jit(solution)/shard_map/broadcast_in_dim | solution.py:42
  3.0 7.6 %all-to-all-start = ((bf16[16,192,384]{2,1,0:T(8,128)(2,1)}), bf16[16,192,384]{2,1,0:T(8,128)(2,1)}, u32[]{:S(2)}, u32[]{:S(2)}) async-start(bf16[16,192,384]{2,1,0:T(8,128)(2,1)} %broadcast_in_dim.4), calls=%async_computation | async-start | bytes 4718592 | tf_op jit(solution)/shard_map/all_to_all | solution.py:42
  10.6 0.0 copy-done.4
  10.6 0.0 copy-start.5
  10.6 0.6 fusion.15
  12.1 52.9 %all-gather.4 = f16[6400,384]{1,0:T(8,128)(2,1)S(1)} all-gather(f16[200,384]{1,0:T(8,128)(2,1)S(1)} %concatenate.9), channel_id=2, replica_groups=mesh['row'=16,'col'=16,'layer'=2] {'col','layer'}, dimensions={0}, use_global_device_ids=true | all-gather | bytes 5068800 | tf_op jit(solution)/shard_map/all_gather | solution.py:43
  65.0 2.2 %copy-done = f16[6400,384]{1,0:T(8,128)(2,1)} copy-done((f16[6400,384]{1,0:T(8,128)(2,1)}, f16[6400,384]{1,0:T(8,128)(2,1)S(1)}, u32[]{:S(2)}) %copy-start) | copy-done | bytes 4915224
  67.2 0.1 copy.55
  67.3 0.0 copy-done.5
  67.3 0.2 broadcast_in_dim.5
  67.5 0.4 reshape.17
  67.8 0.0 copy-start.2
  67.8 0.2 constant_dynamic-slice_fusion.2
  68.0 0.1 copy.56
  68.2 6.1 %multiply_convert_fusion.1 = bf16[32,192,384]{2,1,0:T(8,128)(2,1)} fusion(f16[32,200,384]{2,1,0:T(8,128)(2,1)} %bitcast.38, f32[32]{0:T(128)S(1)} %exponential_bitcast_fusion.1), kind=kLoop, calls=%fused_computation.1 | loop fusion | flops 7077888 | bytes 9437312 | tf_op jit(solution)/shard_map/convert_element_type | solution.py:29
  74.3 0.0 copy-done.2
  74.3 0.0 all-to-all-done
  74.3 5.3 %abs_reduce_fusion = (f32[]{:T(128)}, f32[192,384]{1,0:T(8,128)S(1)}) fusion(f32[384,192]{0,1:T(8,128)S(1)} %copy.56, bf16[16,192,384]{2,1,0:T(8,128)(2,1)} %all-to-all-done, bf16[16,384,384]{2,1,0:T(8,128)(2,1)} %bitcast.42), kind=kOutput, calls=%fused_computation.24 | convolution fusion | flops 906338304 | bytes 7667716 | tf_op jit(solution)/shard_map/kjc,krc->jr/dot_general | solution.py:49
  80.5 2.1 %collective-permute-start = (bf16[16,192,384]{2,1,0:T(8,128)(2,1)}, bf16[16,192,384]{2,1,0:T(8,128)(2,1)}, u32[]{:S(2)}, u32[]{:S(2)}) collective-permute-start(bf16[16,192,384]{2,1,0:T(8,128)(2,1)} %all-to-all-done), channel_id=1, source_target_pairs={{0,1},{1,0},{2,3},{3,2},{4,5},{5,4},{6,7},{7,6},{8,9},{9,8},{10,11... | collective-permute-start | bytes 7077896 | tf_op jit(solution)/shard_map/ppermute | solution.py:45
  82.5 44.4 %all-gather.5 = f16[6400,384]{1,0:T(8,128)(2,1)S(1)} all-gather(f16[200,384]{1,0:T(8,128)(2,1)S(1)} %concatenate.10), channel_id=3, replica_groups=mesh['row'=16,'col'=16,'layer'=2] {'col','layer'}, dimensions={0}, use_global_device_ids=true | all-gather | bytes 5068800 | tf_op jit(solution)/shard_map/all_gather | solution.py:51
  127.0 2.2 %copy-done.1 = f16[6400,384]{1,0:T(8,128)(2,1)} copy-done((f16[6400,384]{1,0:T(8,128)(2,1)}, f16[6400,384]{1,0:T(8,128)(2,1)S(1)}, u32[]{:S(2)}) %copy-start.1) | copy-done | bytes 4915224
  129.2 0.1 copy.57
  129.3 3.9 %multiply_convert_fusion = bf16[32,192,384]{2,1,0:T(8,128)(2,1)S(1)} fusion(f16[32,200,384]{2,1,0:T(8,128)(2,1)} %bitcast.40, f32[32]{0:T(128)S(1)} %exponential_bitcast_fusion), kind=kLoop, calls=%fused_computation | loop fusion | flops 7077888 | bytes 9437312 | tf_op jit(solution)/shard_map/convert_element_type | solution.py:29
  133.2 1.6 %constant_dynamic-slice_fusion.1 = bf16[6144,192]{1,0:T(8,128)(2,1)S(1)} fusion(bf16[6144,384]{1,0:T(8,128)(2,1)S(1)} %bitcast.41, s32[]{:T(128)S(6)} %select_n.23), kind=kLoop, calls=%fused_computation.27 | loop fusion | bytes 4718596 | tf_op jit(solution)/shard_map/dynamic_slice | solution.py:52
  134.8 0.1 copy.58
  134.9 0.0 collective-permute-done
  135.0 2.9 %fusion.9 = f32[192,192]{0,1:T(8,128)S(1)} fusion(bf16[16,384,192]{2,1,0:T(8,128)(2,1)S(1)} %bitcast.44, bf16[16,192,384]{2,1,0:T(8,128)(2,1)} %all-to-all-done, bf16[16,192,384]{2,1,0:T(8,128)(2,1)} %collective-permute-done, pred[]{:T(512)S(6)} %eq.4), kind=kOutput, calls=%fused_computation.12 | convolution fusion | flops 454164480 | bytes 7225345 | tf_op jit(solution)/shard_map/kjc,kcr->jr/dot_general | solution.py:58
  137.8 2.9 %fusion.12 = f32[192,192]{0,1:T(8,128)S(1)} fusion(bf16[16,384,192]{2,1,0:T(8,128)(2,1)S(1)} %bitcast.45, bf16[16,192,384]{2,1,0:T(8,128)(2,1)} %collective-permute-done, bf16[16,192,384]{2,1,0:T(8,128)(2,1)} %all-to-all-done, pred[]{:T(512)S(6)} %eq.4), kind=kOutput, calls=%fused_computation.13 | convolution fusion | flops 454164480 | bytes 7225345 | tf_op jit(solution)/shard_map/kjc,kcr->jr/dot_general | solution.py:58
  140.8 0.8 fusion.20
  (14 shorter events, 0.2 us)
Async XLA Ops:
  1.2 9.4 %copy-start.4 = (bf16[384,384]{1,0:T(8,128)(2,1)S(1)}, bf16[384,384]{1,0:T(8,128)(2,1)}, u32[]{:S(2)}) copy-start(bf16[384,384]{1,0:T(8,128)(2,1)} %param.2) | copy-start | bytes 884740
  3.0 71.3 %all-to-all-start = ((bf16[16,192,384]{2,1,0:T(8,128)(2,1)}), bf16[16,192,384]{2,1,0:T(8,128)(2,1)}, u32[]{:S(2)}, u32[]{:S(2)}) async-start(bf16[16,192,384]{2,1,0:T(8,128)(2,1)} %broadcast_in_dim.4), calls=%async_computation | async-start | bytes 4718592 | tf_op jit(solution)/shard_map/all_to_all | solution.py:42
  10.6 56.6 %copy-start.5 = (s32[6,6]{1,0:T(8,128)S(1)}, s32[6,6]{1,0:T(8,128)}, u32[]{:S(2)}) copy-start(s32[6,6]{1,0:T(8,128)} %param.3) | copy-start | bytes 436
  65.0 2.2 %copy-start = (f16[6400,384]{1,0:T(8,128)(2,1)}, f16[6400,384]{1,0:T(8,128)(2,1)S(1)}, u32[]{:S(2)}) copy-start(f16[6400,384]{1,0:T(8,128)(2,1)S(1)} %all-gather.4) | copy-start | bytes 14745604
  67.8 6.5 %copy-start.2 = (f32[384,384]{1,0:T(8,128)}, f32[384,384]{1,0:T(8,128)S(1)}, u32[]{:S(2)}) copy-start(f32[384,384]{1,0:T(8,128)S(1)} %reshape.17) | copy-start | bytes 1769476
  80.5 54.5 %collective-permute-start = (bf16[16,192,384]{2,1,0:T(8,128)(2,1)}, bf16[16,192,384]{2,1,0:T(8,128)(2,1)}, u32[]{:S(2)}, u32[]{:S(2)}) collective-permute-start(bf16[16,192,384]{2,1,0:T(8,128)(2,1)} %all-to-all-done), channel_id=1, source_target_pairs={{0,1},{1,0},{2,3},{3,2},{4,5},{5,4},{6,7},{7,6},{8,9},{9,8},{10,11... | collective-permute-start | bytes 7077896 | tf_op jit(solution)/shard_map/ppermute | solution.py:45
  127.0 2.2 %copy-start.1 = (f16[6400,384]{1,0:T(8,128)(2,1)}, f16[6400,384]{1,0:T(8,128)(2,1)S(1)}, u32[]{:S(2)}) copy-start(f16[6400,384]{1,0:T(8,128)(2,1)S(1)} %all-gather.5) | copy-start | bytes 14745604
  137.8 3.0 %copy-start.3 = (f32[384,384]{1,0:T(8,128)S(1)}, f32[384,384]{1,0:T(8,128)}, u32[]{:S(2)}) copy-start(f32[384,384]{1,0:T(8,128)} %copy-done.2) | copy-start | bytes 1769476

commit v3 on v1

v3 whole, which is shorter than its diff:
```python
import functools

import jax
import jax.numpy as jnp
from jax import lax
from jax.experimental import pallas as pl
from jax.experimental.pallas import tpu as pltpu
from jax.sharding import PartitionSpec as P

TILE = 64
TOP = 32767.0
POWER = 17
F32, BF16 = jnp.float32, jnp.bfloat16


def encode(values, bound):
    size = jnp.abs(values) * (1.0 / bound)
    level = jnp.exp(jnp.log(jnp.maximum(size, 1e-37)) * (1.0 / POWER)) * TOP + 0.5
    level = jnp.where(size > 1e-36, jnp.minimum(level, TOP), 0.0)
    return jnp.where(values < 0, -level, level).astype(jnp.int32).astype(jnp.int16)


def decode(codes, bound):
    q = codes.astype(jnp.int32).astype(F32)
    s = q * (1.0 / TOP)
    s2 = s * s
    s4 = s2 * s2
    s8 = s4 * s4
    return ((s8 * s8) * (s * bound)).astype(BF16)


def masked_rows(pattern_ref, first, count, columns, transposed):
    lane_tile = lax.broadcasted_iota(jnp.int32, (TILE, columns), 1) // TILE
    out = []
    for i in range(count):
        row = jnp.zeros((TILE, columns), F32)
        for j in range(columns // TILE):
            here = pattern_ref[j, first + i] if transposed else pattern_ref[first + i, j]
            row = jnp.where(lane_tile == j, here.astype(F32), row)
        out.append(row)
    return jnp.concatenate(out, axis=0)


def start_kernel(layer_ref, block_ref, copies_ref, code_ref, turned, *, bound):
    half = code_ref.shape[0]
    turned[...] = block_ref[...].astype(F32).T
    first = pl.multiple_of(layer_ref[0] * half, half)
    mine = turned[pl.ds(first, half), :]
    code_ref[...] = encode(mine, bound)
    for i in range(copies_ref.shape[0]):
        copies_ref[i] = mine.astype(BF16)


def square_kernel(layer_ref, pattern_ref, right_ref, left_ref, code_ref, *, pair, bounds):
    blocks, half, side = right_ref.shape
    total = jnp.zeros((half, side), F32)
    for k in range(0, blocks, pair):
        right = jnp.concatenate([right_ref[k + i] for i in range(pair)], axis=1)
        left = decode(left_ref[k * side : (k + pair) * side, :], bounds[0])
        total += jnp.dot(right, left, preferred_element_type=F32)
    tiles = half // TILE
    mask = masked_rows(pattern_ref, layer_ref[0] * tiles, tiles, side, True)
    squared = (total * mask).astype(BF16).astype(F32)
    code_ref[...] = encode(squared, bounds[1])


def cube_kernel(
    place_ref, pattern_ref, own_ref, other_ref, strip_ref, out_ref, joined, turned, *, pair, bound
):
    layer, col = place_ref[0], place_ref[1]
    blocks, half, side = own_ref.shape
    width = joined.shape[1]
    lanes = pl.ds(pl.multiple_of(layer * (side - width), 128), width)
    totals = [jnp.zeros((half, width), F32), jnp.zeros((half, width), F32)]
    for k in range(0, blocks, pair):
        strip = decode(strip_ref[k * side : (k + pair) * side, lanes], bound)
        for n, ref in enumerate((own_ref, other_ref)):
            right = jnp.concatenate([ref[k + i] for i in range(pair)], axis=1)
            totals[n] += jnp.dot(right, strip, preferred_element_type=F32)
    joined[pl.ds(pl.multiple_of(layer * half, half), half), :] = totals[0]
    joined[pl.ds(pl.multiple_of((1 - layer) * half, half), half), :] = totals[1]
    square = decode(strip_ref[pl.ds(pl.multiple_of(col * side, side), side), lanes], bound)
    turned[...] = (3.0 * square.astype(F32) - 2.0 * joined[...]).T
    skip = side - half - (side - width)
    rows = turned[pl.ds(pl.multiple_of(layer * skip, 8), half), :]
    tiles = half // TILE
    mask = masked_rows(pattern_ref, layer * tiles, tiles, side, False)
    out_ref[...] = (rows * mask).astype(BF16)


def shards(density, product_pattern):
    layers = lax.axis_size("layer")
    layer_pos = lax.axis_index("layer")
    rows, cols = lax.axis_size("row"), lax.axis_size("col")
    side = density.shape[0]
    half = side // layers
    bound = 2.0
    square_bound = 2.0 ** (2 + (side * rows - 1).bit_length() - 1)
    vmem = pl.BlockSpec(memory_space=pltpu.VMEM)
    smem = pl.BlockSpec(memory_space=pltpu.SMEM)
    params = pltpu.CompilerParams(vmem_limit_bytes=56 * 1024 * 1024)
    layer = jnp.reshape(layer_pos, (1,)).astype(jnp.int32)
    place = jnp.stack([layer_pos, lax.axis_index("col")]).astype(jnp.int32)

    copies, code = pl.pallas_call(
        functools.partial(start_kernel, bound=bound),
        out_shape=(
            jax.ShapeDtypeStruct((rows, half, side), BF16),
            jax.ShapeDtypeStruct((half, side), jnp.int16),
        ),
        in_specs=[smem, vmem],
        out_specs=(vmem, vmem),
        scratch_shapes=[pltpu.VMEM((side, side), F32)],
        compiler_params=params,
    )(layer, density)
    right = lax.all_to_all(copies, "row", 0, 0)
    left = lax.all_gather(code, ("col", "layer"), tiled=True)
    code = pl.pallas_call(
        functools.partial(square_kernel, pair=2, bounds=(bound, square_bound)),
        out_shape=jax.ShapeDtypeStruct((half, side), jnp.int16),
        in_specs=[smem, smem, vmem, vmem],
        out_specs=vmem,
        compiler_params=params,
    )(layer, product_pattern, right, left)
    other = lax.ppermute(right, "layer", [(i, layers - 1 - i) for i in range(layers)])
    strip = lax.all_gather(code, ("col", "layer"), tiled=True)
    width = -(-half // 128) * 128
    return pl.pallas_call(
        functools.partial(cube_kernel, pair=2, bound=square_bound),
        out_shape=jax.ShapeDtypeStruct((half, side), BF16),
        in_specs=[smem, smem, vmem, vmem, vmem],
        out_specs=vmem,
        scratch_shapes=[pltpu.VMEM((side, width), F32), pltpu.VMEM((width, side), F32)],
        compiler_params=params,
    )(place, product_pattern, right, other, strip)


def solution(mesh):
    placed = (P("row", "col"), P("row", "col"))
    return jax.shard_map(
        shards, mesh=mesh, in_specs=placed, out_specs=P(("row", "layer"), "col"), check_vma=False
    )
```

time: 272 us -> 129 us (0.47)
  the two profiles are of different devices: /device:TPU:8 before, /device:TPU:1 now
where the time goes in v3:
time: 129 us; the launch traced here: 128 us
  blocking collectives  99.2 us (77%)
  Pallas kernels  17.4 us (13%)
  starting transfers between devices  9.76 us (8%)
  local copies, waits for them, and re-layouts  1.47 us (1%)
    all_gather x1, blocking collectives, shards(): left = lax.all_gather(code, ('col', 'layer'), tiled=True)  53.6 us
    all_gather x1, blocking collectives, shards(): strip = lax.all_gather(code, ('col', 'layer'), tiled=True)  45.5 us
    all_to_all x1, starting transfers between devices, shards(): right = lax.all_to_all(copies, 'row', 0, 0)  7.72 us
    pallas_call x1, Pallas kernels, shards(): pl.pallas_call(functools.partial(square_kernel, pair=2, bounds=(bound, sq...  7.34 us
    pallas_call x1, Pallas kernels, shards(): pl.pallas_call(functools.partial(cube_kernel, pair=2, bound=square_bound)...  7.25 us
    pallas_call x1, Pallas kernels, shards(): pl.pallas_call(functools.partial(start_kernel, bound=bound), out_shape=(j...  2.77 us
  transfers between devices with their start and end apart: 2, of which 0 were waited for; matrix products, arithmetic and copies ran while one was open for 1% of the time, Pallas kernels for 6%

profile of v3, /device:TPU:1, one launch (start us, length us, event | category | flops | bytes accessed | tf_op | source)
XLA Modules:
  0.0 128.4 jit_solution(14059638963985401703)
XLA Ops:
  0.0 2.8 %shard_map.28 = (bf16[16,192,384]{2,1,0:T(8,128)(2,1)}, s16[192,384]{1,0:T(8,128)(2,1)}) custom-call(s32[1]{0:T(128)} %bitcast.layer_ref, bf16[384,384]{1,0:T(8,128)(2,1)} %block_ref.1), custom_call_target="tpu_custom_call" | custom-call | tf_op jit(solution)/shard_map/pallas_call | solution.py:105
  2.8 0.0 copy-start.2
  2.8 7.7 %all-to-all-start = ((bf16[16,192,384]{2,1,0:T(8,128)(2,1)}), bf16[16,192,384]{2,1,0:T(8,128)(2,1)S(1)}, u32[]{:S(2)}, u32[]{:S(2)}) async-start(bf16[16,192,384]{2,1,0:T(8,128)(2,1)} %get-tuple-element.7), calls=%async_computation | async-start | bytes 4718592 | tf_op jit(solution)/shard_map/all_to_all | solution.py:116
  10.5 0.0 copy-done.2
  10.5 53.6 %all-gather.2.left_ref = s16[6144,384]{1,0:T(8,128)(2,1)} all-gather(s16[192,384]{1,0:T(8,128)(2,1)S(1)} %copy-done.2), channel_id=1, replica_groups=mesh['row'=16,'col'=16,'layer'=2] {'col','layer'}, dimensions={0}, use_global_device_ids=true | all-gather | bytes 4866048 | tf_op jit(solution)/shard_map/all_gather | solution.py:117
  64.1 0.0 all-to-all-done.right_ref.own_ref
  64.1 0.0 copy-start
  64.1 2.0 %collective-permute-start = (bf16[16,192,384]{2,1,0:T(8,128)(2,1)S(1)}, bf16[16,192,384]{2,1,0:T(8,128)(2,1)S(1)}, u32[]{:S(2)}, u32[]{:S(2)}) collective-permute-start(bf16[16,192,384]{2,1,0:T(8,128)(2,1)S(1)} %all-to-all-done.right_ref.own_ref), channel_id=1, source_target_pairs={{0,1},{1,0},{2,3},{3,2},{4,5},{5,4},{6,7},{7,6},{8,9},{9,8},{10,11... | collective-permute-start | bytes 7077896 | tf_op jit(solution)/shard_map/ppermute | solution.py:125
  66.2 0.7 pad_add_fusion.place_ref
  66.9 0.0 copy-done
  66.9 7.3 %shard_map.29 = s16[192,384]{1,0:T(8,128)(2,1)} custom-call(s32[1]{0:T(128)} %bitcast.layer_ref, s32[6,6]{1,0:T(8,128)} %pattern_ref.3, bf16[16,192,384]{2,1,0:T(8,128)(2,1)} %copy-done, s16[6144,384]{1,0:T(8,128)(2,1)} %all-gather.2.left_ref), custom_call_target="tpu_custom_call" | custom-call | tf_op jit(solution)/shard_map/pallas_call | solution.py:118
  74.2 45.5 %all-gather.3.strip_ref = s16[6144,384]{1,0:T(8,128)(2,1)} all-gather(s16[192,384]{1,0:T(8,128)(2,1)} %shard_map.29), channel_id=1, replica_groups=mesh['row'=16,'col'=16,'layer'=2] {'col','layer'}, dimensions={0}, use_global_device_ids=true | all-gather | bytes 4866048 | tf_op jit(solution)/shard_map/all_gather | solution.py:126
  119.7 0.0 collective-permute-done.other_ref
  119.7 0.0 copy-start.1
  119.7 1.5 %copy-done.1 = bf16[16,192,384]{2,1,0:T(8,128)(2,1)} copy-done((bf16[16,192,384]{2,1,0:T(8,128)(2,1)}, bf16[16,192,384]{2,1,0:T(8,128)(2,1)S(1)}, u32[]{:S(2)}) %copy-start.1) | copy-done | bytes 2359320
  121.2 7.2 %shard_map.30 = bf16[192,384]{1,0:T(8,128)(2,1)} custom-call(s32[2]{0:T(128)} %pad_add_fusion.place_ref, s32[6,6]{1,0:T(8,128)} %pattern_ref.3, bf16[16,192,384]{2,1,0:T(8,128)(2,1)} %copy-done, bf16[16,192,384]{2,1,0:T(8,128)(2,1)} %copy-done.1, s16[6144,384]{1,0:T(8,128)(2,1)} %all-gather.3.strip_ref), custom_call_target="tpu_custom_call" | custom-call | tf_op jit(solution)/shard_map/pallas_call | solution.py:128
Async XLA Ops:
  2.8 7.7 %copy-start.2 = (s16[192,384]{1,0:T(8,128)(2,1)S(1)}, s16[192,384]{1,0:T(8,128)(2,1)}, u32[]{:S(2)}) copy-start(s16[192,384]{1,0:T(8,128)(2,1)} %get-tuple-element.8) | copy-start | bytes 442372
  2.8 61.4 %all-to-all-start = ((bf16[16,192,384]{2,1,0:T(8,128)(2,1)}), bf16[16,192,384]{2,1,0:T(8,128)(2,1)S(1)}, u32[]{:S(2)}, u32[]{:S(2)}) async-start(bf16[16,192,384]{2,1,0:T(8,128)(2,1)} %get-tuple-element.7), calls=%async_computation | async-start | bytes 4718592 | tf_op jit(solution)/shard_map/all_to_all | solution.py:116
  64.1 2.7 %copy-start = (bf16[16,192,384]{2,1,0:T(8,128)(2,1)}, bf16[16,192,384]{2,1,0:T(8,128)(2,1)S(1)}, u32[]{:S(2)}) copy-start(bf16[16,192,384]{2,1,0:T(8,128)(2,1)S(1)} %all-to-all-done.right_ref.own_ref) | copy-start | bytes 7077892
  64.1 55.6 %collective-permute-start = (bf16[16,192,384]{2,1,0:T(8,128)(2,1)S(1)}, bf16[16,192,384]{2,1,0:T(8,128)(2,1)S(1)}, u32[]{:S(2)}, u32[]{:S(2)}) collective-permute-start(bf16[16,192,384]{2,1,0:T(8,128)(2,1)S(1)} %all-to-all-done.right_ref.own_ref), channel_id=1, source_target_pairs={{0,1},{1,0},{2,3},{3,2},{4,5},{5,4},{6,7},{7,6},{8,9},{9,8},{10,11... | collective-permute-start | bytes 7077896 | tf_op jit(solution)/shard_map/ppermute | solution.py:125
  119.7 1.5 %copy-start.1 = (bf16[16,192,384]{2,1,0:T(8,128)(2,1)}, bf16[16,192,384]{2,1,0:T(8,128)(2,1)S(1)}, u32[]{:S(2)}) copy-start(bf16[16,192,384]{2,1,0:T(8,128)(2,1)S(1)} %collective-permute-done.other_ref) | copy-start | bytes 7077892

commit v4 on v3

v4 whole, which is shorter than its diff:
```python
import functools

import jax
import jax.numpy as jnp
from jax import lax
from jax.experimental import pallas as pl
from jax.experimental.pallas import tpu as pltpu
from jax.sharding import PartitionSpec as P

TILE = 64
STEP = 2.0**-15
POWER = 17
F32, BF16 = jnp.float32, jnp.bfloat16


def encode(values, bound):
    size = jnp.abs(values) * (1.0 / bound)
    level = jnp.exp(jnp.log(jnp.maximum(size, 1e-37)) * (1.0 / POWER)) * (1.0 / STEP) + 0.5
    level = jnp.where(size > 1e-36, jnp.minimum(level, 32767.0), 0.0)
    return jnp.where(values < 0, -level, level).astype(jnp.int32).astype(jnp.int16)


def decode(codes):
    q = codes.astype(jnp.int32).astype(F32)
    s2 = (q * q) * (STEP * STEP)
    s4 = s2 * s2
    s8 = s4 * s4
    return ((s8 * s8) * q).astype(BF16)


def fetch(source, chunks, sems):
    rows = chunks.shape[1]
    copies = [
        pltpu.make_async_copy(source.at[pl.ds(n * rows, rows)], chunks.at[n], sems.at[n])
        for n in range(chunks.shape[0])
    ]
    for copy in copies:
        copy.start()
    return copies


def masked_rows(pattern_ref, first, count, columns, transposed):
    lane_tile = lax.broadcasted_iota(jnp.int32, (TILE, columns), 1) // TILE
    out = []
    for i in range(count):
        row = jnp.zeros((TILE, columns), F32)
        for j in range(columns // TILE):
            here = pattern_ref[j, first + i] if transposed else pattern_ref[first + i, j]
            row = jnp.where(lane_tile == j, here.astype(F32), row)
        out.append(row)
    return jnp.concatenate(out, axis=0)


def start_kernel(layer_ref, block_ref, copies_ref, code_ref, turned, mine, sems, *, bound):
    half = code_ref.shape[0]
    turned[...] = block_ref[...].astype(F32).T
    values = turned[pl.ds(pl.multiple_of(layer_ref[0] * half, half), half), :]
    mine[...] = values.astype(BF16)
    copies = [
        pltpu.make_async_copy(mine, copies_ref.at[n], sems.at[n])
        for n in range(copies_ref.shape[0])
    ]
    for copy in copies:
        copy.start()
    code_ref[...] = encode(values, bound)
    for copy in copies:
        copy.wait()


def square_kernel(
    layer_ref,
    pattern_ref,
    right_ref,
    left_ref,
    code_ref,
    right_chunks,
    left_chunks,
    right_sems,
    left_sems,
    *,
    pair,
    bounds,
):
    half, side = code_ref.shape
    rights = fetch(right_ref, right_chunks, right_sems)
    lefts = fetch(left_ref, left_chunks, left_sems)
    tiles = half // TILE
    mask = masked_rows(pattern_ref, layer_ref[0] * tiles, tiles, side, True)
    total = jnp.zeros((half, side), F32)
    for n in range(len(lefts)):
        lefts[n].wait()
        left = decode(left_chunks[n])
        rights[n].wait()
        right = jnp.concatenate([right_chunks[n, i] for i in range(pair)], axis=1)
        total += jnp.dot(right, left, preferred_element_type=F32)
    squared = (total * (bounds[0] * STEP) * mask).astype(BF16).astype(F32)
    code_ref[...] = encode(squared, bounds[1])


def cube_kernel(
    layer_ref,
    col_ref,
    pattern_ref,
    own_ref,
    other_ref,
    strip_ref,
    out_ref,
    joined,
    turned,
    chunks,
    sems,
    *,
    pair,
    bound,
):
    layer = layer_ref[0]
    blocks, half, side = own_ref.shape
    copies = fetch(other_ref, chunks, sems)
    rows = pair * side
    width = joined.shape[1]
    lanes = pl.ds(pl.multiple_of(layer * (side - width), 128), width)
    totals = [jnp.zeros((half, width), F32), jnp.zeros((half, width), F32)]
    for n in range(blocks // pair):
        strip = decode(strip_ref[n * rows : (n + 1) * rows, lanes])
        own = jnp.concatenate([own_ref[n * pair + i] for i in range(pair)], axis=1)
        totals[0] += jnp.dot(own, strip, preferred_element_type=F32)
        copies[n].wait()
        other = jnp.concatenate([chunks[n, i] for i in range(pair)], axis=1)
        totals[1] += jnp.dot(other, strip, preferred_element_type=F32)
    joined[pl.ds(pl.multiple_of(layer * half, half), half), :] = totals[0]
    joined[pl.ds(pl.multiple_of((1 - layer) * half, half), half), :] = totals[1]
    col = col_ref[0]
    square = decode(strip_ref[pl.ds(pl.multiple_of(col * side, side), side), lanes])
    turned[...] = ((3.0 * square.astype(F32) - 2.0 * joined[...]) * (bound * STEP)).T
    result = turned[pl.ds(pl.multiple_of(layer * (width - half), 8), half), :]
    tiles = half // TILE
    mask = masked_rows(pattern_ref, layer * tiles, tiles, side, False)
    out_ref[...] = (result * mask).astype(BF16)


def shards(density, product_pattern):
    layers = lax.axis_size("layer")
    layer = jnp.reshape(lax.axis_index("layer"), (1,))
    col = jnp.reshape(lax.axis_index("col"), (1,))
    rows, cols = lax.axis_size("row"), lax.axis_size("col")
    side = density.shape[0]
    half = side // layers
    width = -(-half // 128) * 128
    pair = 2
    bound = 2.0
    square_bound = 2.0 ** (2 + (side * rows - 1).bit_length() - 1)
    vmem = pl.BlockSpec(memory_space=pltpu.VMEM)
    smem = pl.BlockSpec(memory_space=pltpu.SMEM)
    hbm = pl.BlockSpec(memory_space=pltpu.HBM)
    claims = [pltpu.CompilerParams(vmem_limit_bytes=n << 20) for n in (56, 56, 24)]
    copies, code = pl.pallas_call(
        functools.partial(start_kernel, bound=bound),
        out_shape=(
            jax.ShapeDtypeStruct((rows, half, side), BF16),
            jax.ShapeDtypeStruct((half, side), jnp.int16),
        ),
        in_specs=[smem, vmem],
        out_specs=(hbm, vmem),
        scratch_shapes=[
            pltpu.VMEM((side, side), F32),
            pltpu.VMEM((half, side), BF16),
            pltpu.SemaphoreType.DMA((rows,)),
        ],
        compiler_params=claims[0],
    )(layer, density)
    right = lax.all_to_all(copies, "row", 0, 0)
    left = lax.all_gather(code, ("col", "layer"), tiled=True)
    right, left = lax.optimization_barrier((right, left))
    code = pl.pallas_call(
        functools.partial(square_kernel, pair=pair, bounds=(bound, square_bound)),
        out_shape=jax.ShapeDtypeStruct((half, side), jnp.int16),
        in_specs=[smem, smem, hbm, hbm],
        out_specs=vmem,
        scratch_shapes=[
            pltpu.VMEM((rows // pair, pair, half, side), BF16),
            pltpu.VMEM((cols // pair, pair * side, side), jnp.int16),
            pltpu.SemaphoreType.DMA((rows // pair,)),
            pltpu.SemaphoreType.DMA((cols // pair,)),
        ],
        compiler_params=claims[1],
    )(layer, product_pattern, right, left)
    other = lax.ppermute(right, "layer", [(i, layers - 1 - i) for i in range(layers)])
    strip = lax.all_gather(code, ("col", "layer"), tiled=True)
    return pl.pallas_call(
        functools.partial(cube_kernel, pair=pair, bound=square_bound),
        out_shape=jax.ShapeDtypeStruct((half, side), BF16),
        in_specs=[smem, smem, smem, vmem, hbm, vmem],
        out_specs=vmem,
        scratch_shapes=[
            pltpu.VMEM((side, width), F32),
            pltpu.VMEM((width, side), F32),
            pltpu.VMEM((rows // pair, pair, half, side), BF16),
            pltpu.SemaphoreType.DMA((rows // pair,)),
        ],
        compiler_params=claims[2],
    )(layer, col, product_pattern, right, other, strip)


def solution(mesh):
    placed = (P("row", "col"), P("row", "col"))
    return jax.shard_map(
        shards, mesh=mesh, in_specs=placed, out_specs=P(("row", "layer"), "col"), check_vma=False
    )
```

time: 129 us -> 127 us (0.984)
  blocking collectives: 99.2 us -> 97.7 us
  local copies, waits for them, and re-layouts: 1.47 us -> 0.02 us
  Pallas kernels: 17.4 us -> 18.7 us
    all_gather x1, blocking collectives: 45.5 us -> 44 us  [shards(): strip = lax.all_gather(code, ('col', 'layer'), tiled=True)]
    unnamed x6 -> x8, local copies, waits for them, and re-layouts: 1.47 us -> 0.02 us
  transfers between devices with their start and end apart: 2 -> 2, of which waited for: 0 -> 0; matrix products, arithmetic and copies ran while one was open for 1% -> 0% of each run, Pallas kernels for 6% -> 8%
where the time goes in v4:
time: 127 us; the launch traced here: 126 us
  blocking collectives  97.7 us (77%)
  Pallas kernels  18.7 us (15%)
  starting transfers between devices  9.77 us (8%)
    all_gather x1, blocking collectives, shards(): left = lax.all_gather(code, ('col', 'layer'), tiled=True)  53.6 us
    all_gather x1, blocking collectives, shards(): strip = lax.all_gather(code, ('col', 'layer'), tiled=True)  44 us
    pallas_call x1, Pallas kernels, shards(): pl.pallas_call(functools.partial(square_kernel, pair=pair, bounds=(bound,...  10.1 us
    all_to_all x1, starting transfers between devices, shards(): right = lax.all_to_all(copies, 'row', 0, 0)  7.73 us
    pallas_call x1, Pallas kernels, shards(): pl.pallas_call(functools.partial(cube_kernel, pair=pair, bound=square_bou...  5.19 us
    pallas_call x1, Pallas kernels, shards(): pl.pallas_call(functools.partial(start_kernel, bound=bound), out_shape=(j...  3.4 us
  transfers between devices with their start and end apart: 2, of which 0 were waited for; matrix products, arithmetic and copies ran while one was open for 0% of the time, Pallas kernels for 8%

profile of v4, /device:TPU:1, one launch (start us, length us, event | category | flops | bytes accessed | tf_op | source)
XLA Modules:
  0.0 126.3 jit_solution(5424146985069422516)
XLA Ops:
  0.0 3.4 %shard_map.28 = (bf16[16,192,384]{2,1,0:T(8,128)(2,1)}, s16[192,384]{1,0:T(8,128)(2,1)}) custom-call(s32[1]{0:T(128)} %bitcast.layer_ref, bf16[384,384]{1,0:T(8,128)(2,1)} %block_ref.1), custom_call_target="tpu_custom_call" | custom-call | tf_op jit(solution)/shard_map/pallas_call | solution.py:156
  3.4 0.0 copy-start.3
  3.4 7.7 %all-to-all-start = ((bf16[16,192,384]{2,1,0:T(8,128)(2,1)}), bf16[16,192,384]{2,1,0:T(8,128)(2,1)S(1)}, u32[]{:S(2)}, u32[]{:S(2)}) async-start(bf16[16,192,384]{2,1,0:T(8,128)(2,1)} %get-tuple-element.9), calls=%async_computation | async-start | bytes 4718592 | tf_op jit(solution)/shard_map/all_to_all | solution.py:171
  11.2 0.0 copy-done.3
  11.2 53.6 %all-gather.2.left_ref = s16[6144,384]{1,0:T(8,128)(2,1)} all-gather(s16[192,384]{1,0:T(8,128)(2,1)S(1)} %copy-done.3), channel_id=1, replica_groups=mesh['row'=16,'col'=16,'layer'=2] {'col','layer'}, dimensions={0}, use_global_device_ids=true | all-gather | bytes 4866048 | tf_op jit(solution)/shard_map/all_gather | solution.py:172
  64.8 0.0 all-to-all-done.right_ref.own_ref
  64.8 0.0 copy-start
  64.8 2.0 %collective-permute-start = (bf16[16,192,384]{2,1,0:T(8,128)(2,1)S(1)}, bf16[16,192,384]{2,1,0:T(8,128)(2,1)}, u32[]{:S(2)}, u32[]{:S(2)}) collective-permute-start(bf16[16,192,384]{2,1,0:T(8,128)(2,1)S(1)} %all-to-all-done.right_ref.own_ref), channel_id=1, source_target_pairs={{0,1},{1,0},{2,3},{3,2},{4,5},{5,4},{6,7},{7,6},{8,9},{9,8},{10,11... | collective-permute-start | bytes 7077896 | tf_op jit(solution)/shard_map/ppermute | solution.py:187
  66.9 0.0 copy-done
  66.9 10.1 %shard_map.29 = s16[192,384]{1,0:T(8,128)(2,1)} custom-call(s32[1]{0:T(128)} %bitcast.layer_ref, s32[6,6]{1,0:T(8,128)} %pattern_ref.3, bf16[16,192,384]{2,1,0:T(8,128)(2,1)} %copy-done, s16[6144,384]{1,0:T(8,128)(2,1)} %all-gather.2.left_ref), custom_call_target="tpu_custom_call" | custom-call | tf_op jit(solution)/shard_map/pallas_call | solution.py:174
  77.0 0.0 copy-start.1
  77.0 0.0 copy-start.2
  77.0 44.0 %all-gather.3.strip_ref = s16[6144,384]{1,0:T(8,128)(2,1)S(1)} all-gather(s16[192,384]{1,0:T(8,128)(2,1)} %shard_map.29), channel_id=1, replica_groups=mesh['row'=16,'col'=16,'layer'=2] {'col','layer'}, dimensions={0}, use_global_device_ids=true | all-gather | bytes 4866048 | tf_op jit(solution)/shard_map/all_gather | solution.py:188
  121.0 0.0 collective-permute-done.other_ref
  121.1 0.0 copy-done.1
  121.1 0.0 copy-done.2
  121.1 5.2 %shard_map.30 = bf16[192,384]{1,0:T(8,128)(2,1)} custom-call(s32[1]{0:T(128)} %bitcast.layer_ref, s32[1]{0:T(128)} %bitcast.1.col_ref, s32[6,6]{1,0:T(8,128)S(1)} %copy-done.2, bf16[16,192,384]{2,1,0:T(8,128)(2,1)S(1)} %copy-done.1, bf16[16,192,384]{2,1,0:T(8,128)(2,1)} %collective-permute-done.other_ref, s16[6144,384]{1,0:T(8,128)(2,1)S(1)} %all-gather.3.strip_ref), custom_call_target="tpu_custom_call" | custom-call | tf_op jit(solution)/shard_map/pallas_call | solution.py:189
Async XLA Ops:
  3.4 7.8 %copy-start.3 = (s16[192,384]{1,0:T(8,128)(2,1)S(1)}, s16[192,384]{1,0:T(8,128)(2,1)}, u32[]{:S(2)}) copy-start(s16[192,384]{1,0:T(8,128)(2,1)} %get-tuple-element.10) | copy-start | bytes 442372
  3.4 61.4 %all-to-all-start = ((bf16[16,192,384]{2,1,0:T(8,128)(2,1)}), bf16[16,192,384]{2,1,0:T(8,128)(2,1)S(1)}, u32[]{:S(2)}, u32[]{:S(2)}) async-start(bf16[16,192,384]{2,1,0:T(8,128)(2,1)} %get-tuple-element.9), calls=%async_computation | async-start | bytes 4718592 | tf_op jit(solution)/shard_map/all_to_all | solution.py:171
  64.8 2.1 %copy-start = (bf16[16,192,384]{2,1,0:T(8,128)(2,1)}, bf16[16,192,384]{2,1,0:T(8,128)(2,1)S(1)}, u32[]{:S(2)}) copy-start(bf16[16,192,384]{2,1,0:T(8,128)(2,1)S(1)} %all-to-all-done.right_ref.own_ref) | copy-start | bytes 7077892
  64.8 56.3 %collective-permute-start = (bf16[16,192,384]{2,1,0:T(8,128)(2,1)S(1)}, bf16[16,192,384]{2,1,0:T(8,128)(2,1)}, u32[]{:S(2)}, u32[]{:S(2)}) collective-permute-start(bf16[16,192,384]{2,1,0:T(8,128)(2,1)S(1)} %all-to-all-done.right_ref.own_ref), channel_id=1, source_target_pairs={{0,1},{1,0},{2,3},{3,2},{4,5},{5,4},{6,7},{7,6},{8,9},{9,8},{10,11... | collective-permute-start | bytes 7077896 | tf_op jit(solution)/shard_map/ppermute | solution.py:187
  77.0 44.1 %copy-start.1 = (bf16[16,192,384]{2,1,0:T(8,128)(2,1)S(1)}, bf16[16,192,384]{2,1,0:T(8,128)(2,1)}, u32[]{:S(2)}) copy-start(bf16[16,192,384]{2,1,0:T(8,128)(2,1)} %copy-done) | copy-start | bytes 7077892
  77.0 44.1 %copy-start.2 = (s32[6,6]{1,0:T(8,128)S(1)}, s32[6,6]{1,0:T(8,128)}, u32[]{:S(2)}) copy-start(s32[6,6]{1,0:T(8,128)} %pattern_ref.3) | copy-start | bytes 436

commit v5 on v4

--- a/solution.py
+++ b/solution.py
@@ -9,18 +9,24 @@
 
 TILE = 64
 STEP = 2.0**-15
-POWER = 17
 F32, BF16 = jnp.float32, jnp.bfloat16
 
 
-def encode(values, bound):
+def encode(values, bound, power):
     size = jnp.abs(values) * (1.0 / bound)
-    level = jnp.exp(jnp.log(jnp.maximum(size, 1e-37)) * (1.0 / POWER)) * (1.0 / STEP) + 0.5
+    level = jnp.exp(jnp.log(jnp.maximum(size, 1e-37)) * (1.0 / power)) * (1.0 / STEP) + 0.5
     level = jnp.where(size > 1e-36, jnp.minimum(level, 32767.0), 0.0)
     return jnp.where(values < 0, -level, level).astype(jnp.int32).astype(jnp.int16)
 
 
-def decode(codes):
+def decode7(codes):
+    q = codes.astype(jnp.int32).astype(F32)
+    q2 = q * q
+    q4 = q2 * q2
+    return ((q4 * q2) * q).astype(BF16)
+
+
+def decode17(codes):
     q = codes.astype(jnp.int32).astype(F32)
     s2 = (q * q) * (STEP * STEP)
     s4 = s2 * s2
@@ -28,15 +34,12 @@
     return ((s8 * s8) * q).astype(BF16)
 
 
-def fetch(source, chunks, sems):
+def chunk_copies(source, chunks, sems):
     rows = chunks.shape[1]
-    copies = [
+    return [
         pltpu.make_async_copy(source.at[pl.ds(n * rows, rows)], chunks.at[n], sems.at[n])
         for n in range(chunks.shape[0])
     ]
-    for copy in copies:
-        copy.start()
-    return copies
 
 
 def masked_rows(pattern_ref, first, count, columns, transposed):
@@ -62,7 +65,7 @@
     ]
     for copy in copies:
         copy.start()
-    code_ref[...] = encode(values, bound)
+    code_ref[...] = encode(values, bound, 7)
     for copy in copies:
         copy.wait()
 
@@ -79,22 +82,27 @@
     left_sems,
     *,
     pair,
+    group,
     bounds,
 ):
     half, side = code_ref.shape
-    rights = fetch(right_ref, right_chunks, right_sems)
-    lefts = fetch(left_ref, left_chunks, left_sems)
+    rights = chunk_copies(right_ref, right_chunks, right_sems)
+    lefts = chunk_copies(left_ref, left_chunks, left_sems)
+    for left_copy, right_copy in zip(lefts, rights):
+        left_copy.start()
+        right_copy.start()
     tiles = half // TILE
     mask = masked_rows(pattern_ref, layer_ref[0] * tiles, tiles, side, True)
     total = jnp.zeros((half, side), F32)
-    for n in range(len(lefts)):
-        lefts[n].wait()
-        left = decode(left_chunks[n])
-        rights[n].wait()
-        right = jnp.concatenate([right_chunks[n, i] for i in range(pair)], axis=1)
-        total += jnp.dot(right, left, preferred_element_type=F32)
-    squared = (total * (bounds[0] * STEP) * mask).astype(BF16).astype(F32)
-    code_ref[...] = encode(squared, bounds[1])
+    for first in range(0, len(lefts), group):
+        for n in range(first, first + group):
+            lefts[n].wait()
+            rights[n].wait()
+        for n in range(first, first + group):
+            right = jnp.concatenate([right_chunks[n, i] for i in range(pair)], axis=1)
+            total += jnp.dot(right, decode7(left_chunks[n]), preferred_element_type=F32)
+    squared = (total * (bounds[0] * STEP**7) * mask).astype(BF16).astype(F32)
+    code_ref[...] = encode(squared, bounds[1], 17)
 
 
 def cube_kernel(
@@ -115,13 +123,15 @@
 ):
     layer = layer_ref[0]
     blocks, half, side = own_ref.shape
-    copies = fetch(other_ref, chunks, sems)
+    copies = chunk_copies(other_ref, chunks, sems)
+    for copy in copies:
+        copy.start()
     rows = pair * side
     width = joined.shape[1]
     lanes = pl.ds(pl.multiple_of(layer * (side - width), 128), width)
     totals = [jnp.zeros((half, width), F32), jnp.zeros((half, width), F32)]
     for n in range(blocks // pair):
-        strip = decode(strip_ref[n * rows : (n + 1) * rows, lanes])
+        strip = decode17(strip_ref[n * rows : (n + 1) * rows, lanes])
         own = jnp.concatenate([own_ref[n * pair + i] for i in range(pair)], axis=1)
         totals[0] += jnp.dot(own, strip, preferred_element_type=F32)
         copies[n].wait()
@@ -130,7 +140,7 @@
     joined[pl.ds(pl.multiple_of(layer * half, half), half), :] = totals[0]
     joined[pl.ds(pl.multiple_of((1 - layer) * half, half), half), :] = totals[1]
     col = col_ref[0]
-    square = decode(strip_ref[pl.ds(pl.multiple_of(col * side, side), side), lanes])
+    square = decode17(strip_ref[pl.ds(pl.multiple_of(col * side, side), side), lanes])
     turned[...] = ((3.0 * square.astype(F32) - 2.0 * joined[...]) * (bound * STEP)).T
     result = turned[pl.ds(pl.multiple_of(layer * (width - half), 8), half), :]
     tiles = half // TILE
@@ -172,7 +182,7 @@
     left = lax.all_gather(code, ("col", "layer"), tiled=True)
     right, left = lax.optimization_barrier((right, left))
     code = pl.pallas_call(
-        functools.partial(square_kernel, pair=pair, bounds=(bound, square_bound)),
+        functools.partial(square_kernel, pair=pair, group=2, bounds=(bound, square_bound)),
         out_shape=jax.ShapeDtypeStruct((half, side), jnp.int16),
         in_specs=[smem, smem, hbm, hbm],
         out_specs=vmem,

time: 127 us -> 122 us (0.961)
  Pallas kernels: 18.7 us -> 14.2 us
    pallas_call x1, Pallas kernels: 10.1 us -> 5.64 us  [shards(): pl.pallas_call(functools.partial(square_kernel, pair=pair, group=2, bound...]
  transfers between devices with their start and end apart: 2 -> 2, of which waited for: 0 -> 0; matrix products, arithmetic and copies ran while one was open for 0% -> 0% of each run, Pallas kernels for 8% -> 5%
where the time goes in v5:
time: 122 us
  blocking collectives  97.7 us (80%)
  Pallas kernels  14.2 us (12%)
  starting transfers between devices  9.77 us (8%)
    all_gather x1, blocking collectives, shards(): left = lax.all_gather(code, ('col', 'layer'), tiled=True)  53.6 us
    all_gather x1, blocking collectives, shards(): strip = lax.all_gather(code, ('col', 'layer'), tiled=True)  44.1 us
    all_to_all x1, starting transfers between devices, shards(): right = lax.all_to_all(copies, 'row', 0, 0)  7.73 us
    pallas_call x1, Pallas kernels, shards(): pl.pallas_call(functools.partial(square_kernel, pair=pair, group=2, bound...  5.64 us
    pallas_call x1, Pallas kernels, shards(): pl.pallas_call(functools.partial(cube_kernel, pair=pair, bound=square_bou...  5.19 us
    pallas_call x1, Pallas kernels, shards(): pl.pallas_call(functools.partial(start_kernel, bound=bound), out_shape=(j...  3.4 us
  transfers between devices with their start and end apart: 2, of which 0 were waited for; matrix products, arithmetic and copies ran while one was open for 0% of the time, Pallas kernels for 5%

profile of v5, /device:TPU:1, one launch (start us, length us, event | category | flops | bytes accessed | tf_op | source)
XLA Modules:
  0.0 121.8 jit_solution(5211417102660028042)
XLA Ops:
  0.0 3.4 %shard_map.28 = (bf16[16,192,384]{2,1,0:T(8,128)(2,1)}, s16[192,384]{1,0:T(8,128)(2,1)}) custom-call(s32[1]{0:T(128)} %bitcast.layer_ref, bf16[384,384]{1,0:T(8,128)(2,1)} %block_ref.1), custom_call_target="tpu_custom_call" | custom-call | tf_op jit(solution)/shard_map/pallas_call | solution.py:166
  3.4 0.0 copy-start.3
  3.4 7.7 %all-to-all-start = ((bf16[16,192,384]{2,1,0:T(8,128)(2,1)}), bf16[16,192,384]{2,1,0:T(8,128)(2,1)S(1)}, u32[]{:S(2)}, u32[]{:S(2)}) async-start(bf16[16,192,384]{2,1,0:T(8,128)(2,1)} %get-tuple-element.9), calls=%async_computation | async-start | bytes 4718592 | tf_op jit(solution)/shard_map/all_to_all | solution.py:181
  11.2 0.0 copy-done.3
  11.2 53.6 %all-gather.2.left_ref = s16[6144,384]{1,0:T(8,128)(2,1)} all-gather(s16[192,384]{1,0:T(8,128)(2,1)S(1)} %copy-done.3), channel_id=1, replica_groups=mesh['row'=16,'col'=16,'layer'=2] {'col','layer'}, dimensions={0}, use_global_device_ids=true | all-gather | bytes 4866048 | tf_op jit(solution)/shard_map/all_gather | solution.py:182
  64.8 0.0 all-to-all-done.right_ref.own_ref
  64.8 0.0 copy-start
  64.8 2.0 %collective-permute-start = (bf16[16,192,384]{2,1,0:T(8,128)(2,1)S(1)}, bf16[16,192,384]{2,1,0:T(8,128)(2,1)}, u32[]{:S(2)}, u32[]{:S(2)}) collective-permute-start(bf16[16,192,384]{2,1,0:T(8,128)(2,1)S(1)} %all-to-all-done.right_ref.own_ref), channel_id=1, source_target_pairs={{0,1},{1,0},{2,3},{3,2},{4,5},{5,4},{6,7},{7,6},{8,9},{9,8},{10,11... | collective-permute-start | bytes 7077896 | tf_op jit(solution)/shard_map/ppermute | solution.py:197
  66.9 0.0 copy-done
  66.9 5.6 %shard_map.29 = s16[192,384]{1,0:T(8,128)(2,1)} custom-call(s32[1]{0:T(128)} %bitcast.layer_ref, s32[6,6]{1,0:T(8,128)} %pattern_ref.3, bf16[16,192,384]{2,1,0:T(8,128)(2,1)} %copy-done, s16[6144,384]{1,0:T(8,128)(2,1)} %all-gather.2.left_ref), custom_call_target="tpu_custom_call" | custom-call | tf_op jit(solution)/shard_map/pallas_call | solution.py:184
  72.5 0.0 copy-start.1
  72.5 0.0 copy-start.2
  72.5 44.1 %all-gather.3.strip_ref = s16[6144,384]{1,0:T(8,128)(2,1)S(1)} all-gather(s16[192,384]{1,0:T(8,128)(2,1)} %shard_map.29), channel_id=1, replica_groups=mesh['row'=16,'col'=16,'layer'=2] {'col','layer'}, dimensions={0}, use_global_device_ids=true | all-gather | bytes 4866048 | tf_op jit(solution)/shard_map/all_gather | solution.py:198
  116.6 0.0 collective-permute-done.other_ref
  116.6 0.0 copy-done.1
  116.6 0.0 copy-done.2
  116.6 5.2 %shard_map.30 = bf16[192,384]{1,0:T(8,128)(2,1)} custom-call(s32[1]{0:T(128)} %bitcast.layer_ref, s32[1]{0:T(128)} %bitcast.1.col_ref, s32[6,6]{1,0:T(8,128)S(1)} %copy-done.2, bf16[16,192,384]{2,1,0:T(8,128)(2,1)S(1)} %copy-done.1, bf16[16,192,384]{2,1,0:T(8,128)(2,1)} %collective-permute-done.other_ref, s16[6144,384]{1,0:T(8,128)(2,1)S(1)} %all-gather.3.strip_ref), custom_call_target="tpu_custom_call" | custom-call | tf_op jit(solution)/shard_map/pallas_call | solution.py:199
Async XLA Ops:
  3.4 7.8 %copy-start.3 = (s16[192,384]{1,0:T(8,128)(2,1)S(1)}, s16[192,384]{1,0:T(8,128)(2,1)}, u32[]{:S(2)}) copy-start(s16[192,384]{1,0:T(8,128)(2,1)} %get-tuple-element.10) | copy-start | bytes 442372
  3.4 61.4 %all-to-all-start = ((bf16[16,192,384]{2,1,0:T(8,128)(2,1)}), bf16[16,192,384]{2,1,0:T(8,128)(2,1)S(1)}, u32[]{:S(2)}, u32[]{:S(2)}) async-start(bf16[16,192,384]{2,1,0:T(8,128)(2,1)} %get-tuple-element.9), calls=%async_computation | async-start | bytes 4718592 | tf_op jit(solution)/shard_map/all_to_all | solution.py:181
  64.8 2.1 %copy-start = (bf16[16,192,384]{2,1,0:T(8,128)(2,1)}, bf16[16,192,384]{2,1,0:T(8,128)(2,1)S(1)}, u32[]{:S(2)}) copy-start(bf16[16,192,384]{2,1,0:T(8,128)(2,1)S(1)} %all-to-all-done.right_ref.own_ref) | copy-start | bytes 7077892
  64.8 51.8 %collective-permute-start = (bf16[16,192,384]{2,1,0:T(8,128)(2,1)S(1)}, bf16[16,192,384]{2,1,0:T(8,128)(2,1)}, u32[]{:S(2)}, u32[]{:S(2)}) collective-permute-start(bf16[16,192,384]{2,1,0:T(8,128)(2,1)S(1)} %all-to-all-done.right_ref.own_ref), channel_id=1, source_target_pairs={{0,1},{1,0},{2,3},{3,2},{4,5},{5,4},{6,7},{7,6},{8,9},{9,8},{10,11... | collective-permute-start | bytes 7077896 | tf_op jit(solution)/shard_map/ppermute | solution.py:197
  72.5 44.1 %copy-start.1 = (bf16[16,192,384]{2,1,0:T(8,128)(2,1)S(1)}, bf16[16,192,384]{2,1,0:T(8,128)(2,1)}, u32[]{:S(2)}) copy-start(bf16[16,192,384]{2,1,0:T(8,128)(2,1)} %copy-done) | copy-start | bytes 7077892
  72.5 44.1 %copy-start.2 = (s32[6,6]{1,0:T(8,128)S(1)}, s32[6,6]{1,0:T(8,128)}, u32[]{:S(2)}) copy-start(s32[6,6]{1,0:T(8,128)} %pattern_ref.3) | copy-start | bytes 436

commit v6 on v5

--- a/solution.py
+++ b/solution.py
@@ -71,36 +71,21 @@
 
 
 def square_kernel(
-    layer_ref,
-    pattern_ref,
-    right_ref,
-    left_ref,
-    code_ref,
-    right_chunks,
-    left_chunks,
-    right_sems,
-    left_sems,
-    *,
-    pair,
-    group,
-    bounds,
+    layer_ref, pattern_ref, right_ref, left_ref, code_ref, chunks, sems, *, pair, group, bounds
 ):
     half, side = code_ref.shape
-    rights = chunk_copies(right_ref, right_chunks, right_sems)
-    lefts = chunk_copies(left_ref, left_chunks, left_sems)
-    for left_copy, right_copy in zip(lefts, rights):
-        left_copy.start()
-        right_copy.start()
+    copies = chunk_copies(left_ref, chunks, sems)
+    for copy in copies:
+        copy.start()
     tiles = half // TILE
     mask = masked_rows(pattern_ref, layer_ref[0] * tiles, tiles, side, True)
     total = jnp.zeros((half, side), F32)
-    for first in range(0, len(lefts), group):
-        for n in range(first, first + group):
-            lefts[n].wait()
-            rights[n].wait()
-        for n in range(first, first + group):
-            right = jnp.concatenate([right_chunks[n, i] for i in range(pair)], axis=1)
-            total += jnp.dot(right, decode7(left_chunks[n]), preferred_element_type=F32)
+    for n in range(len(copies)):
+        if n % group == 0:
+            for copy in copies[n : n + group]:
+                copy.wait()
+        right = jnp.concatenate([right_ref[n * pair + i] for i in range(pair)], axis=1)
+        total += jnp.dot(right, decode7(chunks[n]), preferred_element_type=F32)
     squared = (total * (bounds[0] * STEP**7) * mask).astype(BF16).astype(F32)
     code_ref[...] = encode(squared, bounds[1], 17)
 
@@ -119,6 +104,7 @@
     sems,
     *,
     pair,
+    group,
     bound,
 ):
     layer = layer_ref[0]
@@ -129,16 +115,22 @@
     rows = pair * side
     width = joined.shape[1]
     lanes = pl.ds(pl.multiple_of(layer * (side - width), 128), width)
-    totals = [jnp.zeros((half, width), F32), jnp.zeros((half, width), F32)]
+    total = jnp.zeros((side, width), F32)
     for n in range(blocks // pair):
+        if n % group == 0:
+            for copy in copies[n : n + group]:
+                copy.wait()
         strip = decode17(strip_ref[n * rows : (n + 1) * rows, lanes])
-        own = jnp.concatenate([own_ref[n * pair + i] for i in range(pair)], axis=1)
-        totals[0] += jnp.dot(own, strip, preferred_element_type=F32)
-        copies[n].wait()
-        other = jnp.concatenate([chunks[n, i] for i in range(pair)], axis=1)
-        totals[1] += jnp.dot(other, strip, preferred_element_type=F32)
-    joined[pl.ds(pl.multiple_of(layer * half, half), half), :] = totals[0]
-    joined[pl.ds(pl.multiple_of((1 - layer) * half, half), half), :] = totals[1]
+        both = jnp.concatenate(
+            [
+                jnp.concatenate([own_ref[n * pair + i], chunks[n, i]], axis=0)
+                for i in range(pair)
+            ],
+            axis=1,
+        )
+        total += jnp.dot(both, strip, preferred_element_type=F32)
+    joined[pl.ds(pl.multiple_of(layer * half, half), half), :] = total[:half]
+    joined[pl.ds(pl.multiple_of((1 - layer) * half, half), half), :] = total[half:]
     col = col_ref[0]
     square = decode17(strip_ref[pl.ds(pl.multiple_of(col * side, side), side), lanes])
     turned[...] = ((3.0 * square.astype(F32) - 2.0 * joined[...]) * (bound * STEP)).T
@@ -162,7 +154,7 @@
     vmem = pl.BlockSpec(memory_space=pltpu.VMEM)
     smem = pl.BlockSpec(memory_space=pltpu.SMEM)
     hbm = pl.BlockSpec(memory_space=pltpu.HBM)
-    claims = [pltpu.CompilerParams(vmem_limit_bytes=n << 20) for n in (56, 56, 24)]
+    claims = [pltpu.CompilerParams(vmem_limit_bytes=n << 20) for n in (56, 50, 24)]
     copies, code = pl.pallas_call(
         functools.partial(start_kernel, bound=bound),
         out_shape=(
@@ -184,12 +176,10 @@
     code = pl.pallas_call(
         functools.partial(square_kernel, pair=pair, group=2, bounds=(bound, square_bound)),
         out_shape=jax.ShapeDtypeStruct((half, side), jnp.int16),
-        in_specs=[smem, smem, hbm, hbm],
+        in_specs=[smem, smem, vmem, hbm],
         out_specs=vmem,
         scratch_shapes=[
-            pltpu.VMEM((rows // pair, pair, half, side), BF16),
             pltpu.VMEM((cols // pair, pair * side, side), jnp.int16),
-            pltpu.SemaphoreType.DMA((rows // pair,)),
             pltpu.SemaphoreType.DMA((cols // pair,)),
         ],
         compiler_params=claims[1],
@@ -197,7 +187,7 @@
     other = lax.ppermute(right, "layer", [(i, layers - 1 - i) for i in range(layers)])
     strip = lax.all_gather(code, ("col", "layer"), tiled=True)
     return pl.pallas_call(
-        functools.partial(cube_kernel, pair=pair, bound=square_bound),
+        functools.partial(cube_kernel, pair=pair, group=8, bound=square_bound),
         out_shape=jax.ShapeDtypeStruct((half, side), BF16),
         in_specs=[smem, smem, smem, vmem, hbm, vmem],
         out_specs=vmem,

time: 122 us -> 121 us (level)
  transfers between devices with their start and end apart: 2 -> 2, of which waited for: 0 -> 0; matrix products, arithmetic and copies ran while one was open for 0% -> 0% of each run, Pallas kernels for 5% -> 4%
where the time goes in v6:
time: 121 us; the launch traced here: 120 us
  blocking collectives  97.2 us (80%)
  Pallas kernels  13.4 us (11%)
  starting transfers between devices  9.77 us (8%)
    all_gather x1, blocking collectives, shards(): left = lax.all_gather(code, ('col', 'layer'), tiled=True)  53.6 us
    all_gather x1, blocking collectives, shards(): strip = lax.all_gather(code, ('col', 'layer'), tiled=True)  43.6 us
    all_to_all x1, starting transfers between devices, shards(): right = lax.all_to_all(copies, 'row', 0, 0)  7.73 us
    pallas_call x1, Pallas kernels, shards(): pl.pallas_call(functools.partial(cube_kernel, pair=pair, group=8, bound=s...  5.35 us
    pallas_call x1, Pallas kernels, shards(): pl.pallas_call(functools.partial(square_kernel, pair=pair, group=2, bound...  4.62 us
    pallas_call x1, Pallas kernels, shards(): pl.pallas_call(functools.partial(start_kernel, bound=bound), out_shape=(j...  3.39 us
  transfers between devices with their start and end apart: 2, of which 0 were waited for; matrix products, arithmetic and copies ran while one was open for 0% of the time, Pallas kernels for 4%

profile of v6, /device:TPU:1, one launch (start us, length us, event | category | flops | bytes accessed | tf_op | source)
XLA Modules:
  0.0 120.5 jit_solution(13798212707986339625)
XLA Ops:
  0.0 3.4 %shard_map.28 = (bf16[16,192,384]{2,1,0:T(8,128)(2,1)}, s16[192,384]{1,0:T(8,128)(2,1)}) custom-call(s32[1]{0:T(128)} %bitcast.layer_ref, bf16[384,384]{1,0:T(8,128)(2,1)} %block_ref.1), custom_call_target="tpu_custom_call" | custom-call | tf_op jit(solution)/shard_map/pallas_call | solution.py:158
  3.4 0.0 copy-start.1
  3.4 7.7 %all-to-all-start = ((bf16[16,192,384]{2,1,0:T(8,128)(2,1)}), bf16[16,192,384]{2,1,0:T(8,128)(2,1)S(1)}, u32[]{:S(2)}, u32[]{:S(2)}) async-start(bf16[16,192,384]{2,1,0:T(8,128)(2,1)} %get-tuple-element.9), calls=%async_computation | async-start | bytes 4718592 | tf_op jit(solution)/shard_map/all_to_all | solution.py:173
  11.1 0.0 copy-done.1
  11.2 0.0 copy-start
  11.2 53.6 %all-gather.2.left_ref = s16[6144,384]{1,0:T(8,128)(2,1)} all-gather(s16[192,384]{1,0:T(8,128)(2,1)S(1)} %copy-done.1), channel_id=1, replica_groups=mesh['row'=16,'col'=16,'layer'=2] {'col','layer'}, dimensions={0}, use_global_device_ids=true | all-gather | bytes 4866048 | tf_op jit(solution)/shard_map/all_gather | solution.py:174
  64.8 0.0 all-to-all-done.right_ref.own_ref
  64.8 2.0 %collective-permute-start = (bf16[16,192,384]{2,1,0:T(8,128)(2,1)S(1)}, bf16[16,192,384]{2,1,0:T(8,128)(2,1)}, u32[]{:S(2)}, u32[]{:S(2)}) collective-permute-start(bf16[16,192,384]{2,1,0:T(8,128)(2,1)S(1)} %all-to-all-done.right_ref.own_ref), channel_id=1, source_target_pairs={{0,1},{1,0},{2,3},{3,2},{4,5},{5,4},{6,7},{7,6},{8,9},{9,8},{10,11... | collective-permute-start | bytes 7077896 | tf_op jit(solution)/shard_map/ppermute | solution.py:187
  66.9 0.0 copy-done
  66.9 4.6 %shard_map.29 = s16[192,384]{1,0:T(8,128)(2,1)S(1)} custom-call(s32[1]{0:T(128)} %bitcast.layer_ref, s32[6,6]{1,0:T(8,128)S(1)} %copy-done, bf16[16,192,384]{2,1,0:T(8,128)(2,1)S(1)} %all-to-all-done.right_ref.own_ref, s16[6144,384]{1,0:T(8,128)(2,1)} %all-gather.2.left_ref), custom_call_target="tpu_custom_call" | custom-call | tf_op jit(solution)/shard_map/pallas_call | solution.py:176
  71.5 43.6 %all-gather.3.strip_ref = s16[6144,384]{1,0:T(8,128)(2,1)S(1)} all-gather(s16[192,384]{1,0:T(8,128)(2,1)S(1)} %shard_map.29), channel_id=1, replica_groups=mesh['row'=16,'col'=16,'layer'=2] {'col','layer'}, dimensions={0}, use_global_device_ids=true | all-gather | bytes 4866048 | tf_op jit(solution)/shard_map/all_gather | solution.py:188
  115.1 0.0 collective-permute-done.other_ref
  115.1 5.3 %shard_map.30 = bf16[192,384]{1,0:T(8,128)(2,1)} custom-call(s32[1]{0:T(128)} %bitcast.layer_ref, s32[1]{0:T(128)} %bitcast.1.col_ref, s32[6,6]{1,0:T(8,128)S(1)} %copy-done, bf16[16,192,384]{2,1,0:T(8,128)(2,1)S(1)} %all-to-all-done.right_ref.own_ref, bf16[16,192,384]{2,1,0:T(8,128)(2,1)} %collective-permute-done.other_ref, ...), custom_call_target="tpu_custom_call" | custom-call | tf_op jit(solution)/shard_map/pallas_call | solution.py:189
Async XLA Ops:
  3.4 7.8 %copy-start.1 = (s16[192,384]{1,0:T(8,128)(2,1)S(1)}, s16[192,384]{1,0:T(8,128)(2,1)}, u32[]{:S(2)}) copy-start(s16[192,384]{1,0:T(8,128)(2,1)} %get-tuple-element.10) | copy-start | bytes 442372
  3.4 61.4 %all-to-all-start = ((bf16[16,192,384]{2,1,0:T(8,128)(2,1)}), bf16[16,192,384]{2,1,0:T(8,128)(2,1)S(1)}, u32[]{:S(2)}, u32[]{:S(2)}) async-start(bf16[16,192,384]{2,1,0:T(8,128)(2,1)} %get-tuple-element.9), calls=%async_computation | async-start | bytes 4718592 | tf_op jit(solution)/shard_map/all_to_all | solution.py:173
  11.2 55.7 %copy-start = (s32[6,6]{1,0:T(8,128)S(1)}, s32[6,6]{1,0:T(8,128)}, u32[]{:S(2)}) copy-start(s32[6,6]{1,0:T(8,128)} %pattern_ref.3) | copy-start | bytes 436
  64.8 50.3 %collective-permute-start = (bf16[16,192,384]{2,1,0:T(8,128)(2,1)S(1)}, bf16[16,192,384]{2,1,0:T(8,128)(2,1)}, u32[]{:S(2)}, u32[]{:S(2)}) collective-permute-start(bf16[16,192,384]{2,1,0:T(8,128)(2,1)S(1)} %all-to-all-done.right_ref.own_ref), channel_id=1, source_target_pairs={{0,1},{1,0},{2,3},{3,2},{4,5},{5,4},{6,7},{7,6},{8,9},{9,8},{10,11... | collective-permute-start | bytes 7077896 | tf_op jit(solution)/shard_map/ppermute | solution.py:187

commit v7 on v6

--- a/solution.py
+++ b/solution.py
@@ -104,7 +104,7 @@
     sems,
     *,
     pair,
-    group,
+    lead,
     bound,
 ):
     layer = layer_ref[0]
@@ -115,11 +115,20 @@
     rows = pair * side
     width = joined.shape[1]
     lanes = pl.ds(pl.multiple_of(layer * (side - width), 128), width)
-    total = jnp.zeros((side, width), F32)
-    for n in range(blocks // pair):
-        if n % group == 0:
-            for copy in copies[n : n + group]:
-                copy.wait()
+    strips = []
+    total = jnp.zeros((half, width), F32)
+    for n in range(lead):
+        strips.append(decode17(strip_ref[n * rows : (n + 1) * rows, lanes]))
+        own = jnp.concatenate([own_ref[n * pair + i] for i in range(pair)], axis=1)
+        total += jnp.dot(own, strips[n], preferred_element_type=F32)
+    for copy in copies:
+        copy.wait()
+    others = jnp.zeros((half, width), F32)
+    for n in range(lead):
+        other = jnp.concatenate([chunks[n, i] for i in range(pair)], axis=1)
+        others += jnp.dot(other, strips[n], preferred_element_type=F32)
+    total = jnp.concatenate([total, others], axis=0)
+    for n in range(lead, blocks // pair):
         strip = decode17(strip_ref[n * rows : (n + 1) * rows, lanes])
         both = jnp.concatenate(
             [
@@ -154,11 +163,11 @@
     vmem = pl.BlockSpec(memory_space=pltpu.VMEM)
     smem = pl.BlockSpec(memory_space=pltpu.SMEM)
     hbm = pl.BlockSpec(memory_space=pltpu.HBM)
-    claims = [pltpu.CompilerParams(vmem_limit_bytes=n << 20) for n in (56, 50, 24)]
+    claims = [pltpu.CompilerParams(vmem_limit_bytes=n << 20) for n in (24, 50, 24)]
     copies, code = pl.pallas_call(
         functools.partial(start_kernel, bound=bound),
         out_shape=(
-            jax.ShapeDtypeStruct((rows, half, side), BF16),
+            pltpu.HBM((rows, half, side), BF16),
             jax.ShapeDtypeStruct((half, side), jnp.int16),
         ),
         in_specs=[smem, vmem],
@@ -187,7 +196,7 @@
     other = lax.ppermute(right, "layer", [(i, layers - 1 - i) for i in range(layers)])
     strip = lax.all_gather(code, ("col", "layer"), tiled=True)
     return pl.pallas_call(
-        functools.partial(cube_kernel, pair=pair, group=8, bound=square_bound),
+        functools.partial(cube_kernel, pair=pair, lead=2, bound=square_bound),
         out_shape=jax.ShapeDtypeStruct((half, side), BF16),
         in_specs=[smem, smem, smem, vmem, hbm, vmem],
         out_specs=vmem,

time: 121 us -> 120 us (level)
  Pallas kernels: 13.4 us -> 11.2 us
    pallas_call x2, Pallas kernels: 8.74 us -> 6.56 us  [the longest x1 4.79 us: shards(): pl.pallas_call(functools.partial(cube_kernel, pair=pair, lead=2, bound=sq...]
where the time goes in v7:
time: 120 us; the launch traced here: 119 us
  blocking collectives  97.2 us (81%)
  Pallas kernels  11.2 us (9%)
  starting transfers between devices  9.64 us (8%)
    all_gather x1, blocking collectives, shards(): left = lax.all_gather(code, ('col', 'layer'), tiled=True)  53.6 us
    all_gather x1, blocking collectives, shards(): strip = lax.all_gather(code, ('col', 'layer'), tiled=True)  43.6 us
    all_to_all x1, starting transfers between devices, shards(): right = lax.all_to_all(copies, 'row', 0, 0)  7.6 us
    pallas_call x1, Pallas kernels, shards(): pl.pallas_call(functools.partial(cube_kernel, pair=pair, lead=2, bound=sq...  4.79 us
    pallas_call x1, Pallas kernels, shards(): pl.pallas_call(functools.partial(square_kernel, pair=pair, group=2, bound...  4.62 us
  transfers between devices with their start and end apart: 2, of which 0 were waited for; matrix products, arithmetic and copies ran while one was open for 0% of the time, Pallas kernels for 4%

profile of v7, /device:TPU:1, one launch (start us, length us, event | category | flops | bytes accessed | tf_op | source)
XLA Modules:
  0.0 119.1 jit_solution(10312168945517737374)
XLA Ops:
  0.0 0.0 copy-start
  0.0 1.0 copy-done
  1.0 1.8 %shard_map.28 = (bf16[16,192,384]{2,1,0:T(8,128)(2,1)}, s16[192,384]{1,0:T(8,128)(2,1)S(1)}) custom-call(s32[1]{0:T(128)} %bitcast.layer_ref, bf16[384,384]{1,0:T(8,128)(2,1)S(1)} %copy-done), custom_call_target="tpu_custom_call" | custom-call | tf_op jit(solution)/shard_map/pallas_call | solution.py:167
  2.7 7.6 %all-to-all-start = ((bf16[16,192,384]{2,1,0:T(8,128)(2,1)}), bf16[16,192,384]{2,1,0:T(8,128)(2,1)S(1)}, u32[]{:S(2)}, u32[]{:S(2)}) async-start(bf16[16,192,384]{2,1,0:T(8,128)(2,1)} %get-tuple-element.9), calls=%async_computation | async-start | bytes 4718592 | tf_op jit(solution)/shard_map/all_to_all | solution.py:182
  10.3 0.0 copy-start.1
  10.4 53.6 %all-gather.2.left_ref = s16[6144,384]{1,0:T(8,128)(2,1)} all-gather(s16[192,384]{1,0:T(8,128)(2,1)S(1)} %get-tuple-element.10), channel_id=1, replica_groups=mesh['row'=16,'col'=16,'layer'=2] {'col','layer'}, dimensions={0}, use_global_device_ids=true | all-gather | bytes 4866048 | tf_op jit(solution)/shard_map/all_gather | solution.py:183
  64.0 0.0 all-to-all-done.right_ref.own_ref
  64.0 2.0 %collective-permute-start = (bf16[16,192,384]{2,1,0:T(8,128)(2,1)S(1)}, bf16[16,192,384]{2,1,0:T(8,128)(2,1)}, u32[]{:S(2)}, u32[]{:S(2)}) collective-permute-start(bf16[16,192,384]{2,1,0:T(8,128)(2,1)S(1)} %all-to-all-done.right_ref.own_ref), channel_id=1, source_target_pairs={{0,1},{1,0},{2,3},{3,2},{4,5},{5,4},{6,7},{7,6},{8,9},{9,8},{10,11... | collective-permute-start | bytes 7077896 | tf_op jit(solution)/shard_map/ppermute | solution.py:196
  66.0 0.0 copy-done.1
  66.1 4.6 %shard_map.29 = s16[192,384]{1,0:T(8,128)(2,1)S(1)} custom-call(s32[1]{0:T(128)} %bitcast.layer_ref, s32[6,6]{1,0:T(8,128)S(1)} %copy-done.1, bf16[16,192,384]{2,1,0:T(8,128)(2,1)S(1)} %all-to-all-done.right_ref.own_ref, s16[6144,384]{1,0:T(8,128)(2,1)} %all-gather.2.left_ref), custom_call_target="tpu_custom_call" | custom-call | tf_op jit(solution)/shard_map/pallas_call | solution.py:185
  70.7 43.6 %all-gather.3.strip_ref = s16[6144,384]{1,0:T(8,128)(2,1)S(1)} all-gather(s16[192,384]{1,0:T(8,128)(2,1)S(1)} %shard_map.29), channel_id=1, replica_groups=mesh['row'=16,'col'=16,'layer'=2] {'col','layer'}, dimensions={0}, use_global_device_ids=true | all-gather | bytes 4866048 | tf_op jit(solution)/shard_map/all_gather | solution.py:197
  114.3 0.0 collective-permute-done.other_ref
  114.3 4.8 %shard_map.30 = bf16[192,384]{1,0:T(8,128)(2,1)} custom-call(s32[1]{0:T(128)} %bitcast.layer_ref, s32[1]{0:T(128)} %bitcast.1.col_ref, s32[6,6]{1,0:T(8,128)S(1)} %copy-done.1, bf16[16,192,384]{2,1,0:T(8,128)(2,1)S(1)} %all-to-all-done.right_ref.own_ref, bf16[16,192,384]{2,1,0:T(8,128)(2,1)} %collective-permute-done.other_ref, ...), custom_call_target="tpu_custom_call" | custom-call | tf_op jit(solution)/shard_map/pallas_call | solution.py:198
Async XLA Ops:
  0.0 1.0 copy-start
  2.7 61.2 %all-to-all-start = ((bf16[16,192,384]{2,1,0:T(8,128)(2,1)}), bf16[16,192,384]{2,1,0:T(8,128)(2,1)S(1)}, u32[]{:S(2)}, u32[]{:S(2)}) async-start(bf16[16,192,384]{2,1,0:T(8,128)(2,1)} %get-tuple-element.9), calls=%async_computation | async-start | bytes 4718592 | tf_op jit(solution)/shard_map/all_to_all | solution.py:182
  10.3 55.7 %copy-start.1 = (s32[6,6]{1,0:T(8,128)S(1)}, s32[6,6]{1,0:T(8,128)}, u32[]{:S(2)}) copy-start(s32[6,6]{1,0:T(8,128)} %pattern_ref.3) | copy-start | bytes 436
  64.0 50.3 %collective-permute-start = (bf16[16,192,384]{2,1,0:T(8,128)(2,1)S(1)}, bf16[16,192,384]{2,1,0:T(8,128)(2,1)}, u32[]{:S(2)}, u32[]{:S(2)}) collective-permute-start(bf16[16,192,384]{2,1,0:T(8,128)(2,1)S(1)} %all-to-all-done.right_ref.own_ref), channel_id=1, source_target_pairs={{0,1},{1,0},{2,3},{3,2},{4,5},{5,4},{6,7},{7,6},{8,9},{9,8},{10,11... | collective-permute-start | bytes 7077896 | tf_op jit(solution)/shard_map/ppermute | solution.py:196

commit v8 on v7

--- a/solution.py
+++ b/solution.py
@@ -54,10 +54,17 @@
     return jnp.concatenate(out, axis=0)
 
 
-def start_kernel(layer_ref, block_ref, copies_ref, code_ref, turned, mine, sems, *, bound):
-    half = code_ref.shape[0]
-    turned[...] = block_ref[...].astype(F32).T
-    values = turned[pl.ds(pl.multiple_of(layer_ref[0] * half, half), half), :]
+def start_kernel(
+    layer_ref, block_ref, copies_ref, code_ref, fetched, turned, mine, sems, fetch_sem, *, bound
+):
+    half, side = code_ref.shape
+    width = fetched.shape[1]
+    lanes = pl.ds(pl.multiple_of(layer_ref[0] * (side - width), 128), width)
+    fetch = pltpu.make_async_copy(block_ref.at[:, lanes], fetched, fetch_sem)
+    fetch.start()
+    fetch.wait()
+    turned[...] = fetched[...].astype(F32).T
+    values = turned[pl.ds(pl.multiple_of(layer_ref[0] * (width - half), 8), half), :]
     mine[...] = values.astype(BF16)
     copies = [
         pltpu.make_async_copy(mine, copies_ref.at[n], sems.at[n])
@@ -163,19 +170,21 @@
     vmem = pl.BlockSpec(memory_space=pltpu.VMEM)
     smem = pl.BlockSpec(memory_space=pltpu.SMEM)
     hbm = pl.BlockSpec(memory_space=pltpu.HBM)
-    claims = [pltpu.CompilerParams(vmem_limit_bytes=n << 20) for n in (24, 50, 24)]
+    claims = [pltpu.CompilerParams(vmem_limit_bytes=n << 20) for n in (56, 50, 24)]
     copies, code = pl.pallas_call(
         functools.partial(start_kernel, bound=bound),
         out_shape=(
             pltpu.HBM((rows, half, side), BF16),
-            jax.ShapeDtypeStruct((half, side), jnp.int16),
+            pltpu.VMEM((half, side), jnp.int16),
         ),
-        in_specs=[smem, vmem],
+        in_specs=[smem, hbm],
         out_specs=(hbm, vmem),
         scratch_shapes=[
-            pltpu.VMEM((side, side), F32),
+            pltpu.VMEM((side, width), BF16),
+            pltpu.VMEM((width, side), F32),
             pltpu.VMEM((half, side), BF16),
             pltpu.SemaphoreType.DMA((rows,)),
+            pltpu.SemaphoreType.DMA,
         ],
         compiler_params=claims[0],
     )(layer, density)
@@ -196,7 +205,7 @@
     other = lax.ppermute(right, "layer", [(i, layers - 1 - i) for i in range(layers)])
     strip = lax.all_gather(code, ("col", "layer"), tiled=True)
     return pl.pallas_call(
-        functools.partial(cube_kernel, pair=pair, lead=2, bound=square_bound),
+        functools.partial(cube_kernel, pair=pair, lead=3, bound=square_bound),
         out_shape=jax.ShapeDtypeStruct((half, side), BF16),
         in_specs=[smem, smem, smem, vmem, hbm, vmem],
         out_specs=vmem,

time: 120 us -> 119 us (level)
  no operation moved by 1% of the time
where the time goes in v8:
time: 119 us
  blocking collectives  97.2 us (82%)
  Pallas kernels  12 us (10%)
  starting transfers between devices  9.64 us (8%)
    all_gather x1, blocking collectives, shards(): left = lax.all_gather(code, ('col', 'layer'), tiled=True)  53.6 us
    all_gather x1, blocking collectives, shards(): strip = lax.all_gather(code, ('col', 'layer'), tiled=True)  43.6 us
    all_to_all x1, starting transfers between devices, shards(): right = lax.all_to_all(copies, 'row', 0, 0)  7.6 us
    pallas_call x1, Pallas kernels, shards(): pl.pallas_call(functools.partial(cube_kernel, pair=pair, lead=3, bound=sq...  4.67 us
    pallas_call x1, Pallas kernels, shards(): pl.pallas_call(functools.partial(square_kernel, pair=pair, group=2, bound...  4.62 us
    pallas_call x1, Pallas kernels, shards(): pl.pallas_call(functools.partial(start_kernel, bound=bound), out_shape=(p...  2.68 us
  transfers between devices with their start and end apart: 2, of which 0 were waited for; matrix products, arithmetic and copies ran while one was open for 0% of the time, Pallas kernels for 4%

profile of v8, /device:TPU:1, one launch (start us, length us, event | category | flops | bytes accessed | tf_op | source)
XLA Modules:
  0.0 118.9 jit_solution(16088383694240283113)
XLA Ops:
  0.0 2.7 %shard_map.28 = (bf16[16,192,384]{2,1,0:T(8,128)(2,1)}, s16[192,384]{1,0:T(8,128)(2,1)S(1)}) custom-call(s32[1]{0:T(128)} %bitcast.layer_ref, bf16[384,384]{1,0:T(8,128)(2,1)} %block_ref.1), custom_call_target="tpu_custom_call" | custom-call | tf_op jit(solution)/shard_map/pallas_call | solution.py:174
  2.7 7.6 %all-to-all-start = ((bf16[16,192,384]{2,1,0:T(8,128)(2,1)}), bf16[16,192,384]{2,1,0:T(8,128)(2,1)S(1)}, u32[]{:S(2)}, u32[]{:S(2)}) async-start(bf16[16,192,384]{2,1,0:T(8,128)(2,1)} %get-tuple-element.9), calls=%async_computation | async-start | bytes 4718592 | tf_op jit(solution)/shard_map/all_to_all | solution.py:191
  10.3 0.0 copy-start
  10.3 53.6 %all-gather.2.left_ref = s16[6144,384]{1,0:T(8,128)(2,1)} all-gather(s16[192,384]{1,0:T(8,128)(2,1)S(1)} %get-tuple-element.10), channel_id=1, replica_groups=mesh['row'=16,'col'=16,'layer'=2] {'col','layer'}, dimensions={0}, use_global_device_ids=true | all-gather | bytes 4866048 | tf_op jit(solution)/shard_map/all_gather | solution.py:192
  63.9 0.0 all-to-all-done.right_ref.own_ref
  63.9 2.0 %collective-permute-start = (bf16[16,192,384]{2,1,0:T(8,128)(2,1)S(1)}, bf16[16,192,384]{2,1,0:T(8,128)(2,1)}, u32[]{:S(2)}, u32[]{:S(2)}) collective-permute-start(bf16[16,192,384]{2,1,0:T(8,128)(2,1)S(1)} %all-to-all-done.right_ref.own_ref), channel_id=1, source_target_pairs={{0,1},{1,0},{2,3},{3,2},{4,5},{5,4},{6,7},{7,6},{8,9},{9,8},{10,11... | collective-permute-start | bytes 7077896 | tf_op jit(solution)/shard_map/ppermute | solution.py:205
  66.0 0.0 copy-done
  66.0 4.6 %shard_map.29 = s16[192,384]{1,0:T(8,128)(2,1)S(1)} custom-call(s32[1]{0:T(128)} %bitcast.layer_ref, s32[6,6]{1,0:T(8,128)S(1)} %copy-done, bf16[16,192,384]{2,1,0:T(8,128)(2,1)S(1)} %all-to-all-done.right_ref.own_ref, s16[6144,384]{1,0:T(8,128)(2,1)} %all-gather.2.left_ref), custom_call_target="tpu_custom_call" | custom-call | tf_op jit(solution)/shard_map/pallas_call | solution.py:194
  70.6 43.6 %all-gather.3.strip_ref = s16[6144,384]{1,0:T(8,128)(2,1)S(1)} all-gather(s16[192,384]{1,0:T(8,128)(2,1)S(1)} %shard_map.29), channel_id=1, replica_groups=mesh['row'=16,'col'=16,'layer'=2] {'col','layer'}, dimensions={0}, use_global_device_ids=true | all-gather | bytes 4866048 | tf_op jit(solution)/shard_map/all_gather | solution.py:206
  114.2 0.0 collective-permute-done.other_ref
  114.3 4.7 %shard_map.30 = bf16[192,384]{1,0:T(8,128)(2,1)} custom-call(s32[1]{0:T(128)} %bitcast.layer_ref, s32[1]{0:T(128)} %bitcast.1.col_ref, s32[6,6]{1,0:T(8,128)S(1)} %copy-done, bf16[16,192,384]{2,1,0:T(8,128)(2,1)S(1)} %all-to-all-done.right_ref.own_ref, bf16[16,192,384]{2,1,0:T(8,128)(2,1)} %collective-permute-done.other_ref, ...), custom_call_target="tpu_custom_call" | custom-call | tf_op jit(solution)/shard_map/pallas_call | solution.py:207
Async XLA Ops:
  2.7 61.2 %all-to-all-start = ((bf16[16,192,384]{2,1,0:T(8,128)(2,1)}), bf16[16,192,384]{2,1,0:T(8,128)(2,1)S(1)}, u32[]{:S(2)}, u32[]{:S(2)}) async-start(bf16[16,192,384]{2,1,0:T(8,128)(2,1)} %get-tuple-element.9), calls=%async_computation | async-start | bytes 4718592 | tf_op jit(solution)/shard_map/all_to_all | solution.py:191
  10.3 55.7 %copy-start = (s32[6,6]{1,0:T(8,128)S(1)}, s32[6,6]{1,0:T(8,128)}, u32[]{:S(2)}) copy-start(s32[6,6]{1,0:T(8,128)} %pattern_ref.3) | copy-start | bytes 436
  63.9 50.3 %collective-permute-start = (bf16[16,192,384]{2,1,0:T(8,128)(2,1)S(1)}, bf16[16,192,384]{2,1,0:T(8,128)(2,1)}, u32[]{:S(2)}, u32[]{:S(2)}) collective-permute-start(bf16[16,192,384]{2,1,0:T(8,128)(2,1)S(1)} %all-to-all-done.right_ref.own_ref), channel_id=1, source_target_pairs={{0,1},{1,0},{2,3},{3,2},{4,5},{5,4},{6,7},{7,6},{8,9},{9,8},{10,11... | collective-permute-start | bytes 7077896 | tf_op jit(solution)/shard_map/ppermute | solution.py:205

commit v9 on v8

--- a/solution.py
+++ b/solution.py
@@ -122,6 +122,10 @@
     rows = pair * side
     width = joined.shape[1]
     lanes = pl.ds(pl.multiple_of(layer * (side - width), 128), width)
+    tiles = half // TILE
+    mask = masked_rows(pattern_ref, layer * tiles, tiles, side, False)
+    col = col_ref[0]
+    square = decode17(strip_ref[pl.ds(pl.multiple_of(col * side, side), side), lanes])
     strips = []
     total = jnp.zeros((half, width), F32)
     for n in range(lead):
@@ -147,12 +151,8 @@
         total += jnp.dot(both, strip, preferred_element_type=F32)
     joined[pl.ds(pl.multiple_of(layer * half, half), half), :] = total[:half]
     joined[pl.ds(pl.multiple_of((1 - layer) * half, half), half), :] = total[half:]
-    col = col_ref[0]
-    square = decode17(strip_ref[pl.ds(pl.multiple_of(col * side, side), side), lanes])
     turned[...] = ((3.0 * square.astype(F32) - 2.0 * joined[...]) * (bound * STEP)).T
     result = turned[pl.ds(pl.multiple_of(layer * (width - half), 8), half), :]
-    tiles = half // TILE
-    mask = masked_rows(pattern_ref, layer * tiles, tiles, side, False)
     out_ref[...] = (result * mask).astype(BF16)
 
 

time: 119 us -> 119 us (level)
  no operation moved by 1% of the time
where the time goes in v9:
time: 119 us
  blocking collectives  97.2 us (82%)
  Pallas kernels  12 us (10%)
  starting transfers between devices  9.64 us (8%)
    all_gather x1, blocking collectives, shards(): left = lax.all_gather(code, ('col', 'layer'), tiled=True)  53.6 us
    all_gather x1, blocking collectives, shards(): strip = lax.all_gather(code, ('col', 'layer'), tiled=True)  43.6 us
    all_to_all x1, starting transfers between devices, shards(): right = lax.all_to_all(copies, 'row', 0, 0)  7.6 us
    pallas_call x1, Pallas kernels, shards(): pl.pallas_call(functools.partial(cube_kernel, pair=pair, lead=3, bound=sq...  4.67 us
    pallas_call x1, Pallas kernels, shards(): pl.pallas_call(functools.partial(square_kernel, pair=pair, group=2, bound...  4.62 us
    pallas_call x1, Pallas kernels, shards(): pl.pallas_call(functools.partial(start_kernel, bound=bound), out_shape=(p...  2.68 us
  transfers between devices with their start and end apart: 2, of which 0 were waited for; matrix products, arithmetic and copies ran while one was open for 0% of the time, Pallas kernels for 4%

profile of v9, /device:TPU:1, one launch (start us, length us, event | category | flops | bytes accessed | tf_op | source)
XLA Modules:
  0.0 118.9 jit_solution(14715288695492335247)
XLA Ops:
  0.0 2.7 %shard_map.28 = (bf16[16,192,384]{2,1,0:T(8,128)(2,1)}, s16[192,384]{1,0:T(8,128)(2,1)S(1)}) custom-call(s32[1]{0:T(128)} %bitcast.layer_ref, bf16[384,384]{1,0:T(8,128)(2,1)} %block_ref.1), custom_call_target="tpu_custom_call" | custom-call | tf_op jit(solution)/shard_map/pallas_call | solution.py:174
  2.7 7.6 %all-to-all-start = ((bf16[16,192,384]{2,1,0:T(8,128)(2,1)}), bf16[16,192,384]{2,1,0:T(8,128)(2,1)S(1)}, u32[]{:S(2)}, u32[]{:S(2)}) async-start(bf16[16,192,384]{2,1,0:T(8,128)(2,1)} %get-tuple-element.9), calls=%async_computation | async-start | bytes 4718592 | tf_op jit(solution)/shard_map/all_to_all | solution.py:191
  10.3 0.0 copy-start
  10.3 53.6 %all-gather.2.left_ref = s16[6144,384]{1,0:T(8,128)(2,1)} all-gather(s16[192,384]{1,0:T(8,128)(2,1)S(1)} %get-tuple-element.10), channel_id=1, replica_groups=mesh['row'=16,'col'=16,'layer'=2] {'col','layer'}, dimensions={0}, use_global_device_ids=true | all-gather | bytes 4866048 | tf_op jit(solution)/shard_map/all_gather | solution.py:192
  63.9 0.0 all-to-all-done.right_ref.own_ref
  63.9 2.0 %collective-permute-start = (bf16[16,192,384]{2,1,0:T(8,128)(2,1)S(1)}, bf16[16,192,384]{2,1,0:T(8,128)(2,1)}, u32[]{:S(2)}, u32[]{:S(2)}) collective-permute-start(bf16[16,192,384]{2,1,0:T(8,128)(2,1)S(1)} %all-to-all-done.right_ref.own_ref), channel_id=1, source_target_pairs={{0,1},{1,0},{2,3},{3,2},{4,5},{5,4},{6,7},{7,6},{8,9},{9,8},{10,11... | collective-permute-start | bytes 7077896 | tf_op jit(solution)/shard_map/ppermute | solution.py:205
  66.0 0.0 copy-done
  66.0 4.6 %shard_map.29 = s16[192,384]{1,0:T(8,128)(2,1)S(1)} custom-call(s32[1]{0:T(128)} %bitcast.layer_ref, s32[6,6]{1,0:T(8,128)S(1)} %copy-done, bf16[16,192,384]{2,1,0:T(8,128)(2,1)S(1)} %all-to-all-done.right_ref.own_ref, s16[6144,384]{1,0:T(8,128)(2,1)} %all-gather.2.left_ref), custom_call_target="tpu_custom_call" | custom-call | tf_op jit(solution)/shard_map/pallas_call | solution.py:194
  70.6 43.6 %all-gather.3.strip_ref = s16[6144,384]{1,0:T(8,128)(2,1)S(1)} all-gather(s16[192,384]{1,0:T(8,128)(2,1)S(1)} %shard_map.29), channel_id=1, replica_groups=mesh['row'=16,'col'=16,'layer'=2] {'col','layer'}, dimensions={0}, use_global_device_ids=true | all-gather | bytes 4866048 | tf_op jit(solution)/shard_map/all_gather | solution.py:206
  114.2 0.0 collective-permute-done.other_ref
  114.3 4.7 %shard_map.30 = bf16[192,384]{1,0:T(8,128)(2,1)} custom-call(s32[1]{0:T(128)} %bitcast.layer_ref, s32[1]{0:T(128)} %bitcast.1.col_ref, s32[6,6]{1,0:T(8,128)S(1)} %copy-done, bf16[16,192,384]{2,1,0:T(8,128)(2,1)S(1)} %all-to-all-done.right_ref.own_ref, bf16[16,192,384]{2,1,0:T(8,128)(2,1)} %collective-permute-done.other_ref, ...), custom_call_target="tpu_custom_call" | custom-call | tf_op jit(solution)/shard_map/pallas_call | solution.py:207
Async XLA Ops:
  2.7 61.2 %all-to-all-start = ((bf16[16,192,384]{2,1,0:T(8,128)(2,1)}), bf16[16,192,384]{2,1,0:T(8,128)(2,1)S(1)}, u32[]{:S(2)}, u32[]{:S(2)}) async-start(bf16[16,192,384]{2,1,0:T(8,128)(2,1)} %get-tuple-element.9), calls=%async_computation | async-start | bytes 4718592 | tf_op jit(solution)/shard_map/all_to_all | solution.py:191
  10.3 55.7 %copy-start = (s32[6,6]{1,0:T(8,128)S(1)}, s32[6,6]{1,0:T(8,128)}, u32[]{:S(2)}) copy-start(s32[6,6]{1,0:T(8,128)} %pattern_ref.3) | copy-start | bytes 436
  63.9 50.3 %collective-permute-start = (bf16[16,192,384]{2,1,0:T(8,128)(2,1)S(1)}, bf16[16,192,384]{2,1,0:T(8,128)(2,1)}, u32[]{:S(2)}, u32[]{:S(2)}) collective-permute-start(bf16[16,192,384]{2,1,0:T(8,128)(2,1)S(1)} %all-to-all-done.right_ref.own_ref), channel_id=1, source_target_pairs={{0,1},{1,0},{2,3},{3,2},{4,5},{5,4},{6,7},{7,6},{8,9},{9,8},{10,11... | collective-permute-start | bytes 7077896 | tf_op jit(solution)/shard_map/ppermute | solution.py:205

commit v10 on v8

--- a/solution.py
+++ b/solution.py
@@ -202,7 +202,8 @@
         ],
         compiler_params=claims[1],
     )(layer, product_pattern, right, left)
-    other = lax.ppermute(right, "layer", [(i, layers - 1 - i) for i in range(layers)])
+    sent, code = lax.optimization_barrier((right, code))
+    other = lax.ppermute(sent, "layer", [(i, layers - 1 - i) for i in range(layers)])
     strip = lax.all_gather(code, ("col", "layer"), tiled=True)
     return pl.pallas_call(
         functools.partial(cube_kernel, pair=pair, lead=3, bound=square_bound),

time: 119 us -> 119 us (level)
  transfers between devices with their start and end apart: 2 -> 2, of which waited for: 0 -> 0; matrix products, arithmetic and copies ran while one was open for 0% -> 0% of each run, Pallas kernels for 4% -> 0%
where the time goes in v10:
time: 119 us
  blocking collectives  97.2 us (82%)
  Pallas kernels  12 us (10%)
  starting transfers between devices  9.66 us (8%)
    all_gather x1, blocking collectives, shards(): left = lax.all_gather(code, ('col', 'layer'), tiled=True)  53.6 us
    all_gather x1, blocking collectives, shards(): strip = lax.all_gather(code, ('col', 'layer'), tiled=True)  43.6 us
    all_to_all x1, starting transfers between devices, shards(): right = lax.all_to_all(copies, 'row', 0, 0)  7.6 us
    pallas_call x1, Pallas kernels, shards(): pl.pallas_call(functools.partial(cube_kernel, pair=pair, lead=3, bound=sq...  4.67 us
    pallas_call x1, Pallas kernels, shards(): pl.pallas_call(functools.partial(square_kernel, pair=pair, group=2, bound...  4.62 us
    pallas_call x1, Pallas kernels, shards(): pl.pallas_call(functools.partial(start_kernel, bound=bound), out_shape=(p...  2.68 us
  transfers between devices with their start and end apart: 2, of which 0 were waited for; matrix products, arithmetic and copies ran while one was open for 0% of the time, Pallas kernels for 0%

profile of v10, /device:TPU:1, one launch (start us, length us, event | category | flops | bytes accessed | tf_op | source)
XLA Modules:
  0.0 118.9 jit_solution(6452962941779925173)
XLA Ops:
  0.0 2.7 %shard_map.28 = (bf16[16,192,384]{2,1,0:T(8,128)(2,1)}, s16[192,384]{1,0:T(8,128)(2,1)S(1)}) custom-call(s32[1]{0:T(128)} %bitcast.layer_ref, bf16[384,384]{1,0:T(8,128)(2,1)} %block_ref.1), custom_call_target="tpu_custom_call" | custom-call | tf_op jit(solution)/shard_map/pallas_call | solution.py:174
  2.7 7.6 %all-to-all-start = ((bf16[16,192,384]{2,1,0:T(8,128)(2,1)}), bf16[16,192,384]{2,1,0:T(8,128)(2,1)S(1)}, u32[]{:S(2)}, u32[]{:S(2)}) async-start(bf16[16,192,384]{2,1,0:T(8,128)(2,1)} %get-tuple-element.11), calls=%async_computation | async-start | bytes 4718592 | tf_op jit(solution)/shard_map/all_to_all | solution.py:191
  10.3 0.0 copy-start
  10.3 53.6 %all-gather.2.left_ref = s16[6144,384]{1,0:T(8,128)(2,1)} all-gather(s16[192,384]{1,0:T(8,128)(2,1)S(1)} %get-tuple-element.12), channel_id=1, replica_groups=mesh['row'=16,'col'=16,'layer'=2] {'col','layer'}, dimensions={0}, use_global_device_ids=true | all-gather | bytes 4866048 | tf_op jit(solution)/shard_map/all_gather | solution.py:192
  63.9 0.0 all-to-all-done.right_ref.own_ref
  63.9 0.0 copy-done
  63.9 4.6 %shard_map.29 = s16[192,384]{1,0:T(8,128)(2,1)S(1)} custom-call(s32[1]{0:T(128)} %bitcast.layer_ref, s32[6,6]{1,0:T(8,128)S(1)} %copy-done, bf16[16,192,384]{2,1,0:T(8,128)(2,1)S(1)} %all-to-all-done.right_ref.own_ref, s16[6144,384]{1,0:T(8,128)(2,1)} %all-gather.2.left_ref), custom_call_target="tpu_custom_call" | custom-call | tf_op jit(solution)/shard_map/pallas_call | solution.py:194
  68.6 2.1 %collective-permute-start = (bf16[16,192,384]{2,1,0:T(8,128)(2,1)S(1)}, bf16[16,192,384]{2,1,0:T(8,128)(2,1)}, u32[]{:S(2)}, u32[]{:S(2)}) collective-permute-start(bf16[16,192,384]{2,1,0:T(8,128)(2,1)S(1)} %all-to-all-done.right_ref.own_ref), channel_id=1, source_target_pairs={{0,1},{1,0},{2,3},{3,2},{4,5},{5,4},{6,7},{7,6},{8,9},{9,8},{10,11... | collective-permute-start | bytes 7077896 | tf_op jit(solution)/shard_map/ppermute | solution.py:206
  70.6 43.6 %all-gather.3.strip_ref = s16[6144,384]{1,0:T(8,128)(2,1)S(1)} all-gather(s16[192,384]{1,0:T(8,128)(2,1)S(1)} %shard_map.29), channel_id=1, replica_groups=mesh['row'=16,'col'=16,'layer'=2] {'col','layer'}, dimensions={0}, use_global_device_ids=true | all-gather | bytes 4866048 | tf_op jit(solution)/shard_map/all_gather | solution.py:207
  114.2 0.0 collective-permute-done.other_ref
  114.2 4.7 %shard_map.30 = bf16[192,384]{1,0:T(8,128)(2,1)} custom-call(s32[1]{0:T(128)} %bitcast.layer_ref, s32[1]{0:T(128)} %bitcast.1.col_ref, s32[6,6]{1,0:T(8,128)S(1)} %copy-done, bf16[16,192,384]{2,1,0:T(8,128)(2,1)S(1)} %all-to-all-done.right_ref.own_ref, bf16[16,192,384]{2,1,0:T(8,128)(2,1)} %collective-permute-done.other_ref, ...), custom_call_target="tpu_custom_call" | custom-call | tf_op jit(solution)/shard_map/pallas_call | solution.py:208
Async XLA Ops:
  2.7 61.2 %all-to-all-start = ((bf16[16,192,384]{2,1,0:T(8,128)(2,1)}), bf16[16,192,384]{2,1,0:T(8,128)(2,1)S(1)}, u32[]{:S(2)}, u32[]{:S(2)}) async-start(bf16[16,192,384]{2,1,0:T(8,128)(2,1)} %get-tuple-element.11), calls=%async_computation | async-start | bytes 4718592 | tf_op jit(solution)/shard_map/all_to_all | solution.py:191
  10.3 53.6 %copy-start = (s32[6,6]{1,0:T(8,128)S(1)}, s32[6,6]{1,0:T(8,128)}, u32[]{:S(2)}) copy-start(s32[6,6]{1,0:T(8,128)} %pattern_ref.3) | copy-start | bytes 436
  68.6 45.7 %collective-permute-start = (bf16[16,192,384]{2,1,0:T(8,128)(2,1)S(1)}, bf16[16,192,384]{2,1,0:T(8,128)(2,1)}, u32[]{:S(2)}, u32[]{:S(2)}) collective-permute-start(bf16[16,192,384]{2,1,0:T(8,128)(2,1)S(1)} %all-to-all-done.right_ref.own_ref), channel_id=1, source_target_pairs={{0,1},{1,0},{2,3},{3,2},{4,5},{5,4},{6,7},{7,6},{8,9},{9,8},{10,11... | collective-permute-start | bytes 7077896 | tf_op jit(solution)/shard_map/ppermute | solution.py:206

commit v11 on v8

--- a/solution.py
+++ b/solution.py
@@ -205,7 +205,7 @@
     other = lax.ppermute(right, "layer", [(i, layers - 1 - i) for i in range(layers)])
     strip = lax.all_gather(code, ("col", "layer"), tiled=True)
     return pl.pallas_call(
-        functools.partial(cube_kernel, pair=pair, lead=3, bound=square_bound),
+        functools.partial(cube_kernel, pair=pair, lead=4, bound=square_bound),
         out_shape=jax.ShapeDtypeStruct((half, side), BF16),
         in_specs=[smem, smem, smem, vmem, hbm, vmem],
         out_specs=vmem,

time: 119 us -> 119 us (level)
  no operation moved by 1% of the time
where the time goes in v11:
time: 119 us
  blocking collectives  97.2 us (82%)
  Pallas kernels  11.8 us (10%)
  starting transfers between devices  9.64 us (8%)
    all_gather x1, blocking collectives, shards(): left = lax.all_gather(code, ('col', 'layer'), tiled=True)  53.6 us
    all_gather x1, blocking collectives, shards(): strip = lax.all_gather(code, ('col', 'layer'), tiled=True)  43.6 us
    all_to_all x1, starting transfers between devices, shards(): right = lax.all_to_all(copies, 'row', 0, 0)  7.6 us
    pallas_call x1, Pallas kernels, shards(): pl.pallas_call(functools.partial(square_kernel, pair=pair, group=2, bound...  4.62 us
    pallas_call x1, Pallas kernels, shards(): pl.pallas_call(functools.partial(cube_kernel, pair=pair, lead=4, bound=sq...  4.52 us
    pallas_call x1, Pallas kernels, shards(): pl.pallas_call(functools.partial(start_kernel, bound=bound), out_shape=(p...  2.68 us
  transfers between devices with their start and end apart: 2, of which 0 were waited for; matrix products, arithmetic and copies ran while one was open for 0% of the time, Pallas kernels for 4%

profile of v11, /device:TPU:1, one launch (start us, length us, event | category | flops | bytes accessed | tf_op | source)
XLA Modules:
  0.0 118.8 jit_solution(5709799779276666359)
XLA Ops:
  0.0 2.7 %shard_map.28 = (bf16[16,192,384]{2,1,0:T(8,128)(2,1)}, s16[192,384]{1,0:T(8,128)(2,1)S(1)}) custom-call(s32[1]{0:T(128)} %bitcast.layer_ref, bf16[384,384]{1,0:T(8,128)(2,1)} %block_ref.1), custom_call_target="tpu_custom_call" | custom-call | tf_op jit(solution)/shard_map/pallas_call | solution.py:174
  2.7 7.6 %all-to-all-start = ((bf16[16,192,384]{2,1,0:T(8,128)(2,1)}), bf16[16,192,384]{2,1,0:T(8,128)(2,1)S(1)}, u32[]{:S(2)}, u32[]{:S(2)}) async-start(bf16[16,192,384]{2,1,0:T(8,128)(2,1)} %get-tuple-element.9), calls=%async_computation | async-start | bytes 4718592 | tf_op jit(solution)/shard_map/all_to_all | solution.py:191
  10.3 0.0 copy-start
  10.3 53.6 %all-gather.2.left_ref = s16[6144,384]{1,0:T(8,128)(2,1)} all-gather(s16[192,384]{1,0:T(8,128)(2,1)S(1)} %get-tuple-element.10), channel_id=1, replica_groups=mesh['row'=16,'col'=16,'layer'=2] {'col','layer'}, dimensions={0}, use_global_device_ids=true | all-gather | bytes 4866048 | tf_op jit(solution)/shard_map/all_gather | solution.py:192
  63.9 0.0 all-to-all-done.right_ref.own_ref
  63.9 2.0 %collective-permute-start = (bf16[16,192,384]{2,1,0:T(8,128)(2,1)S(1)}, bf16[16,192,384]{2,1,0:T(8,128)(2,1)}, u32[]{:S(2)}, u32[]{:S(2)}) collective-permute-start(bf16[16,192,384]{2,1,0:T(8,128)(2,1)S(1)} %all-to-all-done.right_ref.own_ref), channel_id=1, source_target_pairs={{0,1},{1,0},{2,3},{3,2},{4,5},{5,4},{6,7},{7,6},{8,9},{9,8},{10,11... | collective-permute-start | bytes 7077896 | tf_op jit(solution)/shard_map/ppermute | solution.py:205
  66.0 0.0 copy-done
  66.0 4.6 %shard_map.29 = s16[192,384]{1,0:T(8,128)(2,1)S(1)} custom-call(s32[1]{0:T(128)} %bitcast.layer_ref, s32[6,6]{1,0:T(8,128)S(1)} %copy-done, bf16[16,192,384]{2,1,0:T(8,128)(2,1)S(1)} %all-to-all-done.right_ref.own_ref, s16[6144,384]{1,0:T(8,128)(2,1)} %all-gather.2.left_ref), custom_call_target="tpu_custom_call" | custom-call | tf_op jit(solution)/shard_map/pallas_call | solution.py:194
  70.6 43.6 %all-gather.3.strip_ref = s16[6144,384]{1,0:T(8,128)(2,1)S(1)} all-gather(s16[192,384]{1,0:T(8,128)(2,1)S(1)} %shard_map.29), channel_id=1, replica_groups=mesh['row'=16,'col'=16,'layer'=2] {'col','layer'}, dimensions={0}, use_global_device_ids=true | all-gather | bytes 4866048 | tf_op jit(solution)/shard_map/all_gather | solution.py:206
  114.2 0.0 collective-permute-done.other_ref
  114.3 4.5 %shard_map.30 = bf16[192,384]{1,0:T(8,128)(2,1)} custom-call(s32[1]{0:T(128)} %bitcast.layer_ref, s32[1]{0:T(128)} %bitcast.1.col_ref, s32[6,6]{1,0:T(8,128)S(1)} %copy-done, bf16[16,192,384]{2,1,0:T(8,128)(2,1)S(1)} %all-to-all-done.right_ref.own_ref, bf16[16,192,384]{2,1,0:T(8,128)(2,1)} %collective-permute-done.other_ref, ...), custom_call_target="tpu_custom_call" | custom-call | tf_op jit(solution)/shard_map/pallas_call | solution.py:207
Async XLA Ops:
  2.7 61.2 %all-to-all-start = ((bf16[16,192,384]{2,1,0:T(8,128)(2,1)}), bf16[16,192,384]{2,1,0:T(8,128)(2,1)S(1)}, u32[]{:S(2)}, u32[]{:S(2)}) async-start(bf16[16,192,384]{2,1,0:T(8,128)(2,1)} %get-tuple-element.9), calls=%async_computation | async-start | bytes 4718592 | tf_op jit(solution)/shard_map/all_to_all | solution.py:191
  10.3 55.7 %copy-start = (s32[6,6]{1,0:T(8,128)S(1)}, s32[6,6]{1,0:T(8,128)}, u32[]{:S(2)}) copy-start(s32[6,6]{1,0:T(8,128)} %pattern_ref.3) | copy-start | bytes 436
  63.9 50.3 %collective-permute-start = (bf16[16,192,384]{2,1,0:T(8,128)(2,1)S(1)}, bf16[16,192,384]{2,1,0:T(8,128)(2,1)}, u32[]{:S(2)}, u32[]{:S(2)}) collective-permute-start(bf16[16,192,384]{2,1,0:T(8,128)(2,1)S(1)} %all-to-all-done.right_ref.own_ref), channel_id=1, source_target_pairs={{0,1},{1,0},{2,3},{3,2},{4,5},{5,4},{6,7},{7,6},{8,9},{9,8},{10,11... | collective-permute-start | bytes 7077896 | tf_op jit(solution)/shard_map/ppermute | solution.py:205

commit v12 on v9

--- a/solution.py
+++ b/solution.py
@@ -205,7 +205,7 @@
     other = lax.ppermute(right, "layer", [(i, layers - 1 - i) for i in range(layers)])
     strip = lax.all_gather(code, ("col", "layer"), tiled=True)
     return pl.pallas_call(
-        functools.partial(cube_kernel, pair=pair, lead=3, bound=square_bound),
+        functools.partial(cube_kernel, pair=pair, lead=2, bound=square_bound),
         out_shape=jax.ShapeDtypeStruct((half, side), BF16),
         in_specs=[smem, smem, smem, vmem, hbm, vmem],
         out_specs=vmem,

time: 119 us -> 119 us (level)
  no operation moved by 1% of the time
where the time goes in v12:
time: 119 us
  blocking collectives  97.2 us (82%)
  Pallas kernels  12.1 us (10%)
  starting transfers between devices  9.64 us (8%)
    all_gather x1, blocking collectives, shards(): left = lax.all_gather(code, ('col', 'layer'), tiled=True)  53.6 us
    all_gather x1, blocking collectives, shards(): strip = lax.all_gather(code, ('col', 'layer'), tiled=True)  43.6 us
    all_to_all x1, starting transfers between devices, shards(): right = lax.all_to_all(copies, 'row', 0, 0)  7.6 us
    pallas_call x1, Pallas kernels, shards(): pl.pallas_call(functools.partial(cube_kernel, pair=pair, lead=2, bound=sq...  4.79 us
    pallas_call x1, Pallas kernels, shards(): pl.pallas_call(functools.partial(square_kernel, pair=pair, group=2, bound...  4.62 us
    pallas_call x1, Pallas kernels, shards(): pl.pallas_call(functools.partial(start_kernel, bound=bound), out_shape=(p...  2.68 us
  transfers between devices with their start and end apart: 2, of which 0 were waited for; matrix products, arithmetic and copies ran while one was open for 0% of the time, Pallas kernels for 4%

profile of v12, /device:TPU:1, one launch (start us, length us, event | category | flops | bytes accessed | tf_op | source)
XLA Modules:
  0.0 119.0 jit_solution(14143382536342871014)
XLA Ops:
  0.0 2.7 %shard_map.28 = (bf16[16,192,384]{2,1,0:T(8,128)(2,1)}, s16[192,384]{1,0:T(8,128)(2,1)S(1)}) custom-call(s32[1]{0:T(128)} %bitcast.layer_ref, bf16[384,384]{1,0:T(8,128)(2,1)} %block_ref.1), custom_call_target="tpu_custom_call" | custom-call | tf_op jit(solution)/shard_map/pallas_call | solution.py:174
  2.7 7.6 %all-to-all-start = ((bf16[16,192,384]{2,1,0:T(8,128)(2,1)}), bf16[16,192,384]{2,1,0:T(8,128)(2,1)S(1)}, u32[]{:S(2)}, u32[]{:S(2)}) async-start(bf16[16,192,384]{2,1,0:T(8,128)(2,1)} %get-tuple-element.9), calls=%async_computation | async-start | bytes 4718592 | tf_op jit(solution)/shard_map/all_to_all | solution.py:191
  10.3 0.0 copy-start
  10.3 53.6 %all-gather.2.left_ref = s16[6144,384]{1,0:T(8,128)(2,1)} all-gather(s16[192,384]{1,0:T(8,128)(2,1)S(1)} %get-tuple-element.10), channel_id=1, replica_groups=mesh['row'=16,'col'=16,'layer'=2] {'col','layer'}, dimensions={0}, use_global_device_ids=true | all-gather | bytes 4866048 | tf_op jit(solution)/shard_map/all_gather | solution.py:192
  63.9 0.0 all-to-all-done.right_ref.own_ref
  63.9 2.0 %collective-permute-start = (bf16[16,192,384]{2,1,0:T(8,128)(2,1)S(1)}, bf16[16,192,384]{2,1,0:T(8,128)(2,1)}, u32[]{:S(2)}, u32[]{:S(2)}) collective-permute-start(bf16[16,192,384]{2,1,0:T(8,128)(2,1)S(1)} %all-to-all-done.right_ref.own_ref), channel_id=1, source_target_pairs={{0,1},{1,0},{2,3},{3,2},{4,5},{5,4},{6,7},{7,6},{8,9},{9,8},{10,11... | collective-permute-start | bytes 7077896 | tf_op jit(solution)/shard_map/ppermute | solution.py:205
  66.0 0.0 copy-done
  66.0 4.6 %shard_map.29 = s16[192,384]{1,0:T(8,128)(2,1)S(1)} custom-call(s32[1]{0:T(128)} %bitcast.layer_ref, s32[6,6]{1,0:T(8,128)S(1)} %copy-done, bf16[16,192,384]{2,1,0:T(8,128)(2,1)S(1)} %all-to-all-done.right_ref.own_ref, s16[6144,384]{1,0:T(8,128)(2,1)} %all-gather.2.left_ref), custom_call_target="tpu_custom_call" | custom-call | tf_op jit(solution)/shard_map/pallas_call | solution.py:194
  70.6 43.6 %all-gather.3.strip_ref = s16[6144,384]{1,0:T(8,128)(2,1)S(1)} all-gather(s16[192,384]{1,0:T(8,128)(2,1)S(1)} %shard_map.29), channel_id=1, replica_groups=mesh['row'=16,'col'=16,'layer'=2] {'col','layer'}, dimensions={0}, use_global_device_ids=true | all-gather | bytes 4866048 | tf_op jit(solution)/shard_map/all_gather | solution.py:206
  114.2 0.0 collective-permute-done.other_ref
  114.3 4.8 %shard_map.30 = bf16[192,384]{1,0:T(8,128)(2,1)} custom-call(s32[1]{0:T(128)} %bitcast.layer_ref, s32[1]{0:T(128)} %bitcast.1.col_ref, s32[6,6]{1,0:T(8,128)S(1)} %copy-done, bf16[16,192,384]{2,1,0:T(8,128)(2,1)S(1)} %all-to-all-done.right_ref.own_ref, bf16[16,192,384]{2,1,0:T(8,128)(2,1)} %collective-permute-done.other_ref, ...), custom_call_target="tpu_custom_call" | custom-call | tf_op jit(solution)/shard_map/pallas_call | solution.py:207
Async XLA Ops:
  2.7 61.2 %all-to-all-start = ((bf16[16,192,384]{2,1,0:T(8,128)(2,1)}), bf16[16,192,384]{2,1,0:T(8,128)(2,1)S(1)}, u32[]{:S(2)}, u32[]{:S(2)}) async-start(bf16[16,192,384]{2,1,0:T(8,128)(2,1)} %get-tuple-element.9), calls=%async_computation | async-start | bytes 4718592 | tf_op jit(solution)/shard_map/all_to_all | solution.py:191
  10.3 55.7 %copy-start = (s32[6,6]{1,0:T(8,128)S(1)}, s32[6,6]{1,0:T(8,128)}, u32[]{:S(2)}) copy-start(s32[6,6]{1,0:T(8,128)} %pattern_ref.3) | copy-start | bytes 436
  63.9 50.3 %collective-permute-start = (bf16[16,192,384]{2,1,0:T(8,128)(2,1)S(1)}, bf16[16,192,384]{2,1,0:T(8,128)(2,1)}, u32[]{:S(2)}, u32[]{:S(2)}) collective-permute-start(bf16[16,192,384]{2,1,0:T(8,128)(2,1)S(1)} %all-to-all-done.right_ref.own_ref), channel_id=1, source_target_pairs={{0,1},{1,0},{2,3},{3,2},{4,5},{5,4},{6,7},{7,6},{8,9},{9,8},{10,11... | collective-permute-start | bytes 7077896 | tf_op jit(solution)/shard_map/ppermute | solution.py:205
